TPU v7x, 256 devices: a whole 4x4x8 slice. The times are simulated.
256 devices in a mesh: sn: 64 (over z, x, core), br: 4 (over y).
Axes of the slice: x: 4, y: 4, z: 8, core: 2. Of those that a mesh axis runs over, the one named last changes fastest.
Arguments:
- anc_inverse: bfloat16 [64, 16, 16, 128, 128], P('sn')
- parent_panel: bfloat16 [64, 2048, 128], P('sn'), may hold values from -0.125 to 0.125
- parent_dinv: bfloat16 [64, 128, 128], P('sn')
- child_route: int32 [1536, 1], P('sn'), may hold values from 0 to 63; in each aligned block of 24 rows (0 to 23, 24 to 47, ...) at most 2 rows name the same one
- child_pattern: int32 [1536, 4], P('sn'), may hold values from 0 to 16, as said below
- child_panel: bfloat16 [1536, 512, 128], P('sn', 'br'), may hold values from -0.625 to 0.625
- child_dinv: bfloat16 [1536, 128, 128], P('sn', 'br')
Outputs:
- parent_below: bfloat16 [64, 2048, 128], P('sn', 'br')
- parent_diag: bfloat16 [64, 128, 128], P('sn', 'br')
- child_column: bfloat16 [1536, 512, 128], P('sn', 'br')
- child_diag: bfloat16 [1536, 128, 128], P('sn', 'br')
Inputs may be any that keep to these rules, and one draw needn't show every extreme that they name: `child_route`: among the 24 children on one index of sn no parent is named more than 2 times, and on some indices one parent is named exactly 2 times. `child_pattern`: each row starts with 0 (the parent's own block row); its other entries are distinct and rising.
All inputs are finite; a program needn't handle non-finite values.
Results may differ from a plain program's by a relative error of at most 0.0043.
Values may be sent and summed in bfloat16 or wider, within the bound.
A program may use at most 192 MiB of HBM per device.

v0:
```python
import jax
import jax.numpy as jnp
from jax import lax
from jax.sharding import PartitionSpec as P


def on_device(
    anc_inverse, parent_panel, parent_dinv, child_route, child_pattern, child_panel, child_dinv
):
    sn_size = lax.axis_size("sn")
    br_size = lax.axis_size("br")
    row_index = lax.axis_index("br")
    block_width = parent_dinv.shape[-1]
    ancestors = anc_inverse.shape[1]
    anc_blocks = anc_inverse[0]
    parent_blocks = parent_panel[0].reshape(ancestors, block_width, block_width)
    row_share = ancestors // br_size
    own_blocks = lax.dynamic_slice_in_dim(anc_blocks, row_index * row_share, row_share, 0)
    own_below = (
        -jnp.einsum("kqab,qbc->kac", own_blocks, parent_blocks, preferred_element_type=jnp.float32)
    ).astype(jnp.bfloat16)
    below_col = lax.all_gather(own_below, "br", axis=0, tiled=True)
    diag_block = (
        parent_dinv[0].astype(jnp.float32)
        - jnp.einsum("kba,kbc->ac", parent_blocks, below_col, preferred_element_type=jnp.float32)
    ).astype(jnp.bfloat16)
    first_row = jnp.concatenate([diag_block[None], jnp.swapaxes(below_col, 1, 2)], axis=0)
    lower_rows = jnp.concatenate([below_col[:, None], anc_blocks], axis=1)
    full_inverse = jnp.concatenate([first_row[None], lower_rows], axis=0)
    diag_share = block_width // br_size
    parent_below = own_below.reshape(1, row_share * block_width, block_width)
    parent_diag = lax.dynamic_slice_in_dim(diag_block, row_index * diag_share, diag_share, 0)[None]
    child_count = child_route.shape[0]
    capacity = max(2, 2 * child_count // sn_size)
    slot_count = sn_size * capacity
    per_row = child_panel.shape[1] // block_width
    panel_blocks = child_panel.reshape(child_count, per_row, block_width, block_width)
    parent_dev = child_route[:, 0]
    onehot = (parent_dev[:, None] == jnp.arange(sn_size, dtype=jnp.int32)[None, :]).astype(
        jnp.int32
    )
    earlier = jnp.cumsum(onehot, axis=0) - onehot
    slot_rank = jnp.sum(earlier * onehot, axis=1)
    slot_place = parent_dev * capacity + slot_rank

    def place_slots(values):
        empty = jnp.zeros((slot_count,) + values.shape[1:], values.dtype)
        return empty.at[slot_place].set(values).reshape((sn_size, capacity) + values.shape[1:])

    full_panel = lax.all_gather(panel_blocks, "br", axis=1, tiled=True)
    pattern_buf = lax.all_to_all(
        place_slots(child_pattern), "sn", split_axis=0, concat_axis=0, tiled=True
    )
    row_pattern = lax.dynamic_slice_in_dim(pattern_buf, row_index * per_row, per_row, 2)
    picked = full_inverse[row_pattern[..., :, None], pattern_buf[..., None, :]]
    result = -jnp.einsum(
        "ncmkab,nckbd->ncmad",
        picked,
        lax.all_to_all(place_slots(full_panel), "sn", split_axis=0, concat_axis=0, tiled=True),
        preferred_element_type=jnp.float32,
    )
    returned = lax.all_to_all(
        result.astype(jnp.bfloat16), "sn", split_axis=0, concat_axis=0, tiled=True
    )
    column = returned.reshape((slot_count, per_row, block_width, block_width))[slot_place]
    diag_term = jnp.einsum(
        "cmba,cmbd->cad", panel_blocks, column, preferred_element_type=jnp.float32
    )
    summed = lax.psum_scatter(diag_term, "br", scatter_dimension=1, tiled=True)
    child_diag = (child_dinv.astype(jnp.float32) - summed).astype(jnp.bfloat16)
    child_column = column.reshape(child_count, per_row * block_width, block_width)
    return (parent_below, parent_diag, child_column, child_diag)


def solution(mesh):
    placed = (
        P("sn", None, None, None, None),
        P("sn", None, None),
        P("sn", None, None),
        P("sn", None),
        P("sn", None),
        P("sn", "br", None),
        P("sn", "br", None),
    )
    return jax.shard_map(
        on_device,
        mesh=mesh,
        in_specs=placed,
        out_specs=(
            P("sn", "br", None),
            P("sn", "br", None),
            P("sn", "br", None),
            P("sn", "br", None),
        ),
        check_vma=False,
    )
```

profile of v0, /device:TPU:1, one launch (start us, length us, event | category | flops | bytes accessed | tf_op | source)
XLA Modules:
  0.0 610.4 jit_solution(2361668456448650290)
XLA Ops:
  7.2 0.7 all-gather.3.cloned.1.call-update
  7.9 0.8 copy.35
  8.7 0.7 fusion.19
  9.5 0.8 select_reduce_fusion
  11.0 1.2 scatter_custom_fusion
  12.2 13.0 %all-to-all-start = ((s32[64,2,4]{2,1,0:T(2,128)}), s32[64,2,4]{2,1,0:T(2,128)S(1)}, u32[]{:S(2)}, u32[]{:S(2)}) async-start(s32[64,2,4]{2,1,0:T(2,128)} %bitcast.19), calls=%async_computation | async-start | bytes 131072 | tf_op jit(solution)/shard_map/all_to_all | solution.py:51
  25.2 30.6 %all-gather.3.cloned.1.call-done = bf16[24,512,128]{2,1,0:T(8,128)(2,1)} async-done(((bf16[24,128,128]{2,1,0:T(8,128)(2,1)}), bf16[24,512,128]{2,1,0:T(8,128)(2,1)}) %all-gather.3.cloned.1.call-update) | async-done | bytes 3145744 | tf_op jit(solution)/shard_map/all_gather | solution.py:50
  55.8 6.3 %broadcast_in_dim.42 = bf16[128,4,128,128]{3,2,1,0:T(8,128)(2,1)} broadcast(bf16[]{:T(256)} %constant.5.clone.1), dimensions={} | broadcast | bytes 16777218 | tf_op jit(solution)/shard_map/broadcast_in_dim | solution.py:47
  62.0 8.7 %scatter_fusion = bf16[128,4,128,128]{3,2,1,0:T(8,128)(2,1)} fusion(bf16[128,4,128,128]{3,2,1,0:T(8,128)(2,1)} %broadcast_in_dim.42, s32[24]{0:T(128)S(1)} %fusion.24, bf16[24,4,128,128]{3,2,1,0:T(8,128)(2,1)} %bitcast.88), kind=kCustom, calls=%fused_computation.3 | custom fusion | bytes 9437280 | tf_op jit(solution)/shard_map/scatter | solution.py:48
  70.7 11.1 %all-to-all-start.1 = ((bf16[64,2,4,128,128]{4,3,2,1,0:T(8,128)(2,1)}), bf16[64,2,4,128,128]{4,3,2,1,0:T(8,128)(2,1)}, u32[]{:S(2)}, u32[]{:S(2)}) async-start(bf16[64,2,4,128,128]{4,3,2,1,0:T(8,128)(2,1)} %bitcast.83), calls=%async_computation.1 | async-start | bytes 33554432 | tf_op jit(solution)/shard_map/all_to_all | solution.py:59
  81.8 2.3 fusion.11
  84.1 11.1 %all_gather.6 = bf16[16,128,128]{2,1,0:T(8,128)(2,1)S(1)} all-gather(bf16[4,128,128]{2,1,0:T(8,128)(2,1)S(1)} %fusion.11), channel_id=1, replica_groups=mesh['sn'=64,'br'=4] {'br'}, dimensions={0}, use_global_device_ids=true | all-gather | bytes 655360 | tf_op jit(solution)/shard_map/all_gather | solution.py:22
  96.0 8.2 %maximum_maximum_fusion = bf16[17,17,128,128]{3,2,1,0:T(8,128)(2,1)} fusion(bf16[16,16,128,128]{3,2,1,0:T(8,128)(2,1)} %bitcast.87, bf16[16,1,128,128]{3,2,1,0:T(8,128)(2,1)S(1)} %bitcast.86, bf16[1,17,128,128]{3,2,1,0:T(8,128)(2,1)S(1)} %copy.34), kind=kLoop, calls=%fused_computation.4 | loop fusion | flops 9469952 | bytes 18939904 | tf_op jit(solution)/shard_map/concatenate | solution.py:29
  104.8 14.5 %gather_fusion = bf16[512,128,128]{2,1,0:T(8,128)(2,1)} fusion(bf16[17,17,128,128]{3,2,1,0:T(8,128)(2,1)} %maximum_maximum_fusion, s32[512]{0:T(512)S(1)} %reshape.77), kind=kCustom, calls=%fused_computation | custom fusion | bytes 33558528 | tf_op jit(solution)/shard_map/gather | solution.py:55
  119.3 326.5 %all-to-all-done.1 = bf16[64,2,4,128,128]{4,3,2,1,0:T(8,128)(2,1)} async-done(((bf16[64,2,4,128,128]{4,3,2,1,0:T(8,128)(2,1)}), bf16[64,2,4,128,128]{4,3,2,1,0:T(8,128)(2,1)}, u32[]{:S(2)}, u32[]{:S(2)}) %all-to-all-start.1) | async-done | bytes 16777248 | tf_op jit(solution)/shard_map/all_to_all | solution.py:59
  445.9 15.1 %fusion.1 = bf16[64,2,1,128,128]{4,3,1,2,0:T(8,128)(2,1)} fusion(bf16[64,2,4,128,128]{4,3,2,1,0:T(8,128)(2,1)} %bitcast.84, bf16[64,2,4,128,128]{4,3,2,1,0:T(8,128)(2,1)} %all-to-all-done.1), kind=kOutput, calls=%fused_computation.7 | convolution fusion | flops 2151677952 | bytes 37748736 | tf_op jit(solution)/shard_map/ncmkab,nckbd->ncmad/dot_general | solution.py:56
  460.9 15.3 %all-to-all-start.2 = ((bf16[64,2,1,128,128]{4,3,1,2,0:T(8,128)(2,1)}), bf16[64,2,1,128,128]{4,3,1,2,0:T(8,128)(2,1)}, u32[]{:S(2)}, u32[]{:S(2)}) async-start(bf16[64,2,1,128,128]{4,3,1,2,0:T(8,128)(2,1)} %fusion.1), calls=%async_computation.2 | async-start | bytes 8388608 | tf_op jit(solution)/shard_map/all_to_all | solution.py:62
  476.3 94.3 %all-to-all-done.2 = bf16[64,2,1,128,128]{4,3,1,2,0:T(8,128)(2,1)} async-done(((bf16[64,2,1,128,128]{4,3,1,2,0:T(8,128)(2,1)}), bf16[64,2,1,128,128]{4,3,1,2,0:T(8,128)(2,1)}, u32[]{:S(2)}, u32[]{:S(2)}) %all-to-all-start.2) | async-done | bytes 4194336 | tf_op jit(solution)/shard_map/all_to_all | solution.py:62
  570.7 3.7 gather_fusion.1
  574.4 1.6 convolution_bitcast_fusion
  576.0 1.6 copy.42
  578.3 23.5 %reduce-scatter.2.cloned.1.call-done = f32[24,32,128]{2,0,1:T(8,128)} async-done(((f32[24,128,128]{2,0,1:T(8,128)}), f32[24,32,128]{2,0,1:T(8,128)}) %reduce-scatter.2.cloned.1.call-update) | async-done | bytes 393232 | tf_op jit(solution)/shard_map/reduce_scatter | solution.py:69
  601.8 1.1 subtract_convert_fusion
  602.9 0.7 copy.43
  (34 shorter events, 2.9 us)
Async XLA Ops:
  7.2 74.6 %copy-start = (bf16[1,2048,128]{2,1,0:T(8,128)(2,1)S(1)}, bf16[1,2048,128]{2,1,0:T(8,128)(2,1)}, u32[]{:S(2)}) copy-start(bf16[1,2048,128]{2,1,0:T(8,128)(2,1)} %param.8) | copy-start | bytes 1572868
  7.2 48.6 %all-gather.3.cloned.1.call-start = ((), (), s32[]{:S(2)}) async-start(), calls=%async_computation.5 | async-start | bytes 3932160 | tf_op jit(solution)/shard_map/all_gather | solution.py:50
  12.2 58.5 %all-to-all-start = ((s32[64,2,4]{2,1,0:T(2,128)}), s32[64,2,4]{2,1,0:T(2,128)S(1)}, u32[]{:S(2)}, u32[]{:S(2)}) async-start(s32[64,2,4]{2,1,0:T(2,128)} %bitcast.19), calls=%async_computation | async-start | bytes 131072 | tf_op jit(solution)/shard_map/all_to_all | solution.py:51
  70.7 24.5 %copy-start.5 = (bf16[1,128,128]{2,1,0:T(8,128)(2,1)S(1)}, bf16[1,128,128]{2,1,0:T(8,128)(2,1)}, u32[]{:S(2)}) copy-start(bf16[1,128,128]{2,1,0:T(8,128)(2,1)} %param.9) | copy-start | bytes 98308
  70.7 375.2 %all-to-all-start.1 = ((bf16[64,2,4,128,128]{4,3,2,1,0:T(8,128)(2,1)}), bf16[64,2,4,128,128]{4,3,2,1,0:T(8,128)(2,1)}, u32[]{:S(2)}, u32[]{:S(2)}) async-start(bf16[64,2,4,128,128]{4,3,2,1,0:T(8,128)(2,1)} %bitcast.83), calls=%async_computation.1 | async-start | bytes 33554432 | tf_op jit(solution)/shard_map/all_to_all | solution.py:59
  84.1 20.1 %copy-start.4 = (bf16[4,128,128]{2,1,0:T(8,128)(2,1)}, bf16[4,128,128]{2,1,0:T(8,128)(2,1)S(1)}, u32[]{:S(2)}) copy-start(bf16[4,128,128]{2,1,0:T(8,128)(2,1)S(1)} %fusion.11) | copy-start | bytes 393220
  445.9 157.7 %copy-start.1 = (bf16[1,2048,128]{2,1,0:T(8,128)(2,1)S(1)}, bf16[1,2048,128]{2,1,0:T(8,128)(2,1)}, u32[]{:S(2)}) copy-start(bf16[1,2048,128]{2,1,0:T(8,128)(2,1)} %param.8) | copy-start | bytes 1572868
  460.9 113.5 %copy-start.2 = (bf16[24,128,128]{2,1,0:T(8,128)(2,1)S(1)}, bf16[24,128,128]{2,1,0:T(8,128)(2,1)}, u32[]{:S(2)}) copy-start(bf16[24,128,128]{2,1,0:T(8,128)(2,1)} %param.12) | copy-start | bytes 2359300
  460.9 140.9 %copy-start.3 = (bf16[24,32,128]{2,1,0:T(8,128)(2,1)S(1)}, bf16[24,32,128]{2,1,0:T(8,128)(2,1)}, u32[]{:S(2)}) copy-start(bf16[24,32,128]{2,1,0:T(8,128)(2,1)} %param.13) | copy-start | bytes 589828
  460.9 109.8 %all-to-all-start.2 = ((bf16[64,2,1,128,128]{4,3,1,2,0:T(8,128)(2,1)}), bf16[64,2,1,128,128]{4,3,1,2,0:T(8,128)(2,1)}, u32[]{:S(2)}, u32[]{:S(2)}) async-start(bf16[64,2,1,128,128]{4,3,1,2,0:T(8,128)(2,1)} %fusion.1), calls=%async_computation.2 | async-start | bytes 8388608 | tf_op jit(solution)/shard_map/all_to_all | solution.py:62
  476.3 125.5 %reduce-scatter.2.cloned.1.call-start = ((), (), s32[]{:S(2)}) async-start(), calls=%async_computation.4 | async-start | bytes 1966080 | tf_op jit(solution)/shard_map/reduce_scatter | solution.py:69
Sparse Core Ops, SparseCore 0:
  9.8 45.8 all-gather.2
  577.8 23.9 reduce-scatter.1
where the time goes:
time: 611 us; the launch traced here: 610 us
  waiting for transfers between devices  476 us (78%)
  starting transfers between devices  39.5 us (6%)
  local copies, waits for them, and re-layouts  39.1 us (6%)
  matrix products  19.3 us (3%)
  between operations  14.2 us (2%)
  other arithmetic  11.6 us (2%)
  blocking collectives  11.1 us (2%)
    all_to_all x1, waiting for transfers between devices, on_device(): lax.all_to_all(place_slots(full_panel), 'sn', split_axis=0, concat_axis=0...  327 us
    all_to_all x1, waiting for transfers between devices, on_device(): lax.all_to_all(result.astype(jnp.bfloat16), 'sn', split_axis=0, concat_ax...  94.3 us
    all_gather x1, waiting for transfers between devices, on_device(): full_panel = lax.all_gather(panel_blocks, 'br', axis=1, tiled=True)  30.6 us
    reduce_scatter x1, waiting for transfers between devices, on_device(): summed = lax.psum_scatter(diag_term, 'br', scatter_dimension=1, tiled=True)  23.5 us
    all_to_all x1, starting transfers between devices, on_device(): lax.all_to_all(result.astype(jnp.bfloat16), 'sn', split_axis=0, concat_ax...  15.3 us
    dot_general x1, matrix products, on_device(): jnp.einsum('ncmkab,nckbd->ncmad', picked, lax.all_to_all(place_slots(full...  15.1 us
    gather x1, local copies, waits for them, and re-layouts, on_device(): picked = full_inverse[row_pattern[..., :, None], pattern_buf[..., None, :]]  14.5 us
    all_to_all x1, starting transfers between devices, on_device(): lax.all_to_all(place_slots(child_pattern), 'sn', split_axis=0, concat_axi...  13 us
  transfers between devices with their start and end apart: 5, of which 4 were waited for; matrix products, arithmetic and copies ran while one was open for 8% of the time, Pallas kernels for 0%

commit v1 on v0

v1 whole, which is shorter than its diff:
```python
import functools

import jax
import jax.numpy as jnp
from jax import lax
from jax.experimental import pallas as pl
from jax.experimental.pallas import tpu as pltpu
from jax.sharding import PartitionSpec as P

NZ = 8
NXC = 8
NB = 4
CAP = 2
MESH = pl.DeviceIdType.MESH
BF16 = jnp.bfloat16
F32 = jnp.float32


def place():
    sn = lax.axis_index("sn")
    return lax.div(sn, NXC), lax.rem(sn, NXC), lax.axis_index("br")


def greet():
    z, xc, k = place()
    barrier = pltpu.get_barrier_semaphore()

    def along_z(d, carry):
        pl.semaphore_signal(
            barrier, inc=1, device_id=(lax.rem(z + d, NZ) * NXC + xc, k), device_id_type=MESH
        )
        return carry

    def in_plane(o, carry):
        other = lax.rem(xc + lax.div(o, NB), NXC)
        pl.semaphore_signal(
            barrier,
            inc=1,
            device_id=(z * NXC + other, lax.rem(k + lax.rem(o, NB), NB)),
            device_id_type=MESH,
        )
        return carry

    lax.fori_loop(1, NZ, along_z, 0)
    lax.fori_loop(1, NXC * NB, in_plane, 0)
    pl.semaphore_wait(barrier, NZ - 1 + NXC * NB - 1)


def send_kernel(
    slots, z_child, x_pick, panel, x_out, z_send, x_send, z_got, zs_sem, zr_sem, xs_sem, xr_sem
):
    z, xc, k = place()
    greet()

    def z_copy(dz):
        return pltpu.make_async_remote_copy(
            src_ref=z_send.at[dz],
            dst_ref=z_got[dz],
            send_sem=zs_sem.at[dz],
            recv_sem=zr_sem.at[dz],
            device_id=(lax.rem(z + dz, NZ) * NXC + xc, k),
            device_id_type=MESH,
        )

    for dz in (1, 7, 2, 6, 3, 5, 4):

        def fill(j, carry, dz=dz):
            z_send[dz, j] = panel[z_child[dz, j]]
            return carry

        lax.fori_loop(0, slots, fill, 0)
        z_copy(dz).start()

    def own(j, carry):
        z_got[0][j] = panel[z_child[0, j]]
        return carry

    lax.fori_loop(0, slots, own, 0)

    for dz in (0, 1, 7, 2, 6, 3, 5, 4):
        if dz:
            z_copy(dz).wait_recv()
        half, target = dz // NB, dz % NB

        def forward(o, carry, dz=dz, half=half, target=target):
            other = lax.rem(xc + o, NXC)
            for rank in range(CAP):
                x_send[dz * NXC + other, rank] = z_got[dz][x_pick[dz, other * CAP + rank]]
            here = jnp.logical_and(o == 0, k == target)

            @pl.when(here)
            def _():
                pltpu.make_async_copy(
                    x_send.at[dz * NXC + other], x_out.at[half, xc, k], xr_sem
                ).start()

            @pl.when(jnp.logical_not(here))
            def _():
                pltpu.make_async_remote_copy(
                    src_ref=x_send.at[dz * NXC + other],
                    dst_ref=x_out.at[half, xc, k],
                    send_sem=xs_sem,
                    recv_sem=xr_sem,
                    device_id=(z * NXC + other, target),
                    device_id_type=MESH,
                ).start()

            return carry

        lax.fori_loop(0, NXC, forward, 0)

    for dz in range(1, NZ):
        z_copy(dz).wait_send()
    remote = pl.ds(0, NZ * NXC - NZ // NB)
    pltpu.make_async_copy(x_send.at[remote], x_send.at[remote], xs_sem).wait()
    pltpu.make_async_copy(x_out, x_out, xr_sem).wait()


def send_children(slots, ident, z_child, x_pick, panel_blocks):
    width = panel_blocks.shape[-1]
    block = (width, width)
    smem = pl.BlockSpec(memory_space=pltpu.SMEM)
    return pl.pallas_call(
        functools.partial(send_kernel, slots),
        out_shape=jax.ShapeDtypeStruct((NZ // NB, NXC, NB, CAP) + block, BF16),
        in_specs=[smem, smem, pl.BlockSpec(memory_space=pltpu.VMEM)],
        out_specs=pl.BlockSpec(memory_space=pl.ANY),
        scratch_shapes=[
            pltpu.VMEM((NZ, slots) + block, BF16),
            pltpu.VMEM((NZ * NXC, CAP) + block, BF16),
            [pltpu.VMEM((slots,) + block, BF16) for _ in range(NZ)],
            pltpu.SemaphoreType.DMA((NZ,)),
            pltpu.SemaphoreType.DMA((NZ,)),
            pltpu.SemaphoreType.DMA,
            pltpu.SemaphoreType.DMA,
        ],
        compiler_params=pltpu.CompilerParams(
            collective_id=ident, has_side_effects=True, vmem_limit_bytes=40 * 2**20
        ),
    )(z_child, x_pick, panel_blocks)


def return_kernel(
    slots, z_pick, child_slot, y, column, z_back, z_home, y_got, ys_sem, yr_sem, zs_sem, zr_sem
):
    z, xc, k = place()
    greet()

    for dz in (4, 3, 5, 2, 6, 1, 7, 0):
        half = dz // NB

        @pl.when(k == dz % NB)
        def _(dz=dz, half=half):
            def scatter(o, carry):
                other = lax.rem(xc + lax.div(o, NB), NXC)
                row = lax.rem(k + lax.rem(o, NB), NB)

                @pl.when(o == 0)
                def _():
                    pltpu.make_async_copy(
                        y.at[half, other, row], y_got[dz].at[pl.ds(xc * CAP, CAP)], yr_sem.at[dz]
                    ).start()

                @pl.when(o > 0)
                def _():
                    pltpu.make_async_remote_copy(
                        src_ref=y.at[half, other, row],
                        dst_ref=y_got[dz].at[pl.ds(xc * CAP, CAP)],
                        send_sem=ys_sem,
                        recv_sem=yr_sem.at[dz],
                        device_id=(z * NXC + other, row),
                        device_id_type=MESH,
                    ).start()

                return carry

            lax.fori_loop(0, NXC * NB, scatter, 0)

    def z_copy(dz):
        return pltpu.make_async_remote_copy(
            src_ref=z_back.at[dz],
            dst_ref=z_home.at[pl.ds(dz * slots, slots)],
            send_sem=zs_sem.at[dz],
            recv_sem=zr_sem.at[dz],
            device_id=(lax.rem(z + NZ - dz, NZ) * NXC + xc, k),
            device_id_type=MESH,
        )

    for dz in (4, 3, 5, 2, 6, 1, 7, 0):
        pltpu.make_async_copy(y_got[dz], y_got[dz], yr_sem.at[dz]).wait()

        def pack(j, carry, dz=dz):
            if dz:
                z_back[dz, j] = y_got[dz][z_pick[dz, j]]
            else:
                z_home[j] = y_got[dz][z_pick[dz, j]]
            return carry

        lax.fori_loop(0, slots, pack, 0)
        if dz:
            z_copy(dz).start()

    for dz in range(1, NZ):
        z_copy(dz).wait_recv()

    def unpack(i, carry):
        column[i] = z_home[child_slot[i]]
        return carry

    lax.fori_loop(0, column.shape[0], unpack, 0)
    for dz in range(1, NZ):
        z_copy(dz).wait_send()
    sent = NXC * NB - 1
    for half in range(NZ // NB):
        flat = y.at[half, pl.ds(0, NXC - 1)]
        pltpu.make_async_copy(flat, flat, ys_sem).wait()
        last = y.at[half, NXC - 1, pl.ds(0, sent - (NXC - 1) * NB)]
        pltpu.make_async_copy(last, last, ys_sem).wait()


def return_children(slots, ident, z_pick, child_slot, y):
    block = y.shape[-2:]
    smem = pl.BlockSpec(memory_space=pltpu.SMEM)
    count = child_slot.shape[0]
    return pl.pallas_call(
        functools.partial(return_kernel, slots),
        out_shape=jax.ShapeDtypeStruct((count,) + block, BF16),
        in_specs=[smem, smem, pl.BlockSpec(memory_space=pl.ANY)],
        out_specs=pl.BlockSpec(memory_space=pltpu.VMEM),
        scratch_shapes=[
            pltpu.VMEM((NZ, slots) + block, BF16),
            pltpu.VMEM((NZ * slots,) + block, BF16),
            [pltpu.VMEM((NXC * CAP,) + block, BF16) for _ in range(NZ)],
            pltpu.SemaphoreType.DMA,
            pltpu.SemaphoreType.DMA((NZ,)),
            pltpu.SemaphoreType.DMA((NZ,)),
            pltpu.SemaphoreType.DMA((NZ,)),
        ],
        compiler_params=pltpu.CompilerParams(
            collective_id=ident, has_side_effects=True, vmem_limit_bytes=40 * 2**20
        ),
    )(z_pick, child_slot, y)


def parent_kernel(
    pattern, anc, parent_blocks, dinv, x, below_out, diag_out, y, full, sem
):
    ancestors, width = parent_blocks.shape[0], parent_blocks.shape[-1]
    row = lax.axis_index("br")
    for k in range(ancestors):
        pltpu.make_async_copy(
            anc.at[k], full.at[k + 1, pl.ds(1, ancestors)], sem.at[k]
        ).start()
    diag = dinv[...].astype(F32)
    for k in range(ancestors):
        pltpu.make_async_copy(
            anc.at[k], full.at[k + 1, pl.ds(1, ancestors)], sem.at[k]
        ).wait()
        total = jnp.zeros((width, width), F32)
        for l in range(0, ancestors, 4):
            left = jnp.concatenate([full[k + 1, 1 + l + i] for i in range(4)], axis=1)
            right = jnp.concatenate([parent_blocks[l + i] for i in range(4)], axis=0)
            total += jnp.dot(left, right, preferred_element_type=F32)
        total = (-total).astype(BF16)
        full[k + 1, 0] = total
        full[0, k + 1] = total.T
        diag -= lax.dot_general(
            parent_blocks[k], total, (((0,), (0,)), ((), ())), preferred_element_type=F32
        )
    full[0, 0] = diag.astype(BF16)
    share = ancestors // NB
    for i in range(share):
        below_out[i] = full[1 + row * share + i, 0]
    diag_out[...] = full[0, 0, pl.ds(row * (width // NB), width // NB)]

    def child(n, carry):
        group, rank = lax.div(n, CAP), lax.rem(n, CAP)
        half, xc = lax.div(group, NXC), lax.rem(group, NXC)
        spot = [pattern[n, k] for k in range(NB)]
        right = jnp.concatenate([x[half, xc, l, rank] for l in range(NB)], axis=0)
        for k in range(NB):
            left = jnp.concatenate([full[spot[k], spot[l]] for l in range(NB)], axis=1)
            y[half, xc, k, rank] = (-jnp.dot(left, right, preferred_element_type=F32)).astype(BF16)
        return carry

    lax.fori_loop(0, NZ // NB * NXC * CAP, child, 0)


def parent_step(pattern, anc, parent_blocks, dinv, x):
    ancestors, width = parent_blocks.shape[0], parent_blocks.shape[-1]
    vmem = pl.BlockSpec(memory_space=pltpu.VMEM)
    return pl.pallas_call(
        parent_kernel,
        out_shape=(
            jax.ShapeDtypeStruct((ancestors // NB, width, width), BF16),
            jax.ShapeDtypeStruct((width // NB, width), BF16),
            jax.ShapeDtypeStruct(x.shape, BF16),
        ),
        in_specs=[
            pl.BlockSpec(memory_space=pltpu.SMEM),
            pl.BlockSpec(memory_space=pl.ANY),
            vmem,
            vmem,
            vmem,
        ],
        out_specs=(vmem, vmem, vmem),
        scratch_shapes=[
            pltpu.VMEM((ancestors + 1, ancestors + 1, width, width), BF16),
            pltpu.SemaphoreType.DMA((ancestors,)),
        ],
        compiler_params=pltpu.CompilerParams(vmem_limit_bytes=40 * 2**20),
    )(pattern, anc, parent_blocks, dinv, x)


def tables(child_route, child_pattern):
    z, xc, row = place()
    count = child_route.shape[0]
    meta = jnp.concatenate([child_route, child_pattern], axis=1).reshape(-1)
    meta = lax.all_gather(meta, "sn").reshape(NZ, NXC, count, -1)
    route, pattern = meta[..., 0], meta[..., 1:]
    goal = route // NXC
    earlier = jnp.tri(count, k=-1, dtype=jnp.bool_)
    spot = jnp.sum(((goal[..., :, None] == goal[..., None, :]) & earlier).astype(jnp.int32), -1)
    rank = jnp.sum(((route[..., :, None] == route[..., None, :]) & earlier).astype(jnp.int32), -1)
    fullest = jnp.max(spot) + 1
    most = NXC * CAP

    def own(values):
        return lax.dynamic_slice(values, (z, xc, 0), (1, 1, count))[0, 0]

    step = lax.rem(own(goal) - z + NZ, NZ)
    own_spot = own(spot)
    steps = jnp.arange(NZ, dtype=jnp.int32)
    places = jnp.arange(most, dtype=jnp.int32)
    hit = (step == steps[:, None, None]) & (own_spot == places[:, None])
    z_child = jnp.sum(jnp.where(hit, jnp.arange(count, dtype=jnp.int32), 0), -1)

    sources = lax.rem(z - steps + NZ, NZ)

    def column_of(values):
        return lax.dynamic_index_in_dim(values, xc, 1, keepdims=False)[sources]

    mine = column_of(goal) == z
    target = (column_of(route) % NXC) * CAP + column_of(rank)
    via = column_of(spot)
    hit = (mine & True)[:, None] & (target[:, None] == places[:, None])
    x_pick = jnp.sum(jnp.where(hit, via[:, None], 0), -1)
    hit = mine[:, None] & (via[:, None] == places[:, None])
    z_pick = jnp.sum(jnp.where(hit, target[:, None], 0), -1)

    parts = sources.reshape(NZ // NB, NB)[:, row]
    here = (route == z * NXC + xc)[parts]
    hit = here[:, :, None] & (rank[parts][:, :, None] == jnp.arange(CAP)[:, None])
    child_spots = jnp.sum(jnp.where(hit[..., None], pattern[parts][:, :, None], 0), -2)
    return fullest, z_child, x_pick, z_pick, step, own_spot, child_spots.reshape(-1, NB)


def on_device(
    anc_inverse, parent_panel, parent_dinv, child_route, child_pattern, child_panel, child_dinv
):
    width = parent_dinv.shape[-1]
    ancestors = anc_inverse.shape[1]
    count = child_route.shape[0]
    few, most = NXC, NXC * CAP
    panel_blocks = child_panel.reshape(count, width, width)
    parent_blocks = parent_panel[0].reshape(ancestors, width, width)
    fullest, z_child, x_pick, z_pick, step, own_spot, child_spots = tables(
        child_route, child_pattern
    )
    fits = fullest <= few
    x = lax.cond(
        fits,
        functools.partial(send_children, few, 1),
        functools.partial(send_children, most, 2),
        z_child,
        x_pick,
        panel_blocks,
    )
    below, diag, y = parent_step(child_spots, anc_inverse[0], parent_blocks, parent_dinv[0], x)
    column = lax.cond(
        fits,
        lambda a, b, c, d: return_children(few, 3, a, b * few + c, d),
        lambda a, b, c, d: return_children(most, 4, a, b * most + c, d),
        z_pick,
        step,
        own_spot,
        y,
    )
    term = jnp.einsum("cba,cbd->cad", panel_blocks, column, preferred_element_type=F32)
    summed = lax.psum_scatter(term, "br", scatter_dimension=1, tiled=True)
    child_diag = (child_dinv.astype(F32) - summed).astype(BF16)
    return (below.reshape(1, -1, width), diag[None], column, child_diag)


def solution(mesh):
    placed = (
        P("sn", None, None, None, None),
        P("sn", None, None),
        P("sn", None, None),
        P("sn", None),
        P("sn", None),
        P("sn", "br", None),
        P("sn", "br", None),
    )
    return jax.shard_map(
        on_device,
        mesh=mesh,
        in_specs=placed,
        out_specs=(
            P("sn", "br", None),
            P("sn", "br", None),
            P("sn", "br", None),
            P("sn", "br", None),
        ),
        check_vma=False,
    )
```

time: 611 us -> 281 us (0.46)
  waiting for transfers between devices: 476 us -> 31.3 us
  Pallas kernels: 0 us -> 172 us
  starting transfers between devices: 39.5 us -> 0.04 us
  blocking collectives: 11.1 us -> 44 us
  local copies, waits for them, and re-layouts: 39.1 us -> 11.5 us
  matrix products: 19.3 us -> 0.43 us
    all_to_all x3 -> x0, waiting for transfers between devices: 421 us -> none  [the longest x1 327 us: on_device(): lax.all_to_all(place_slots(full_panel), 'sn', split_axis=0, concat_axis=0...]
    pallas_call x0 -> x3, Pallas kernels: none -> 172 us  [the longest x1 78.6 us: send_children(): pl.pallas_call(functools.partial(send_kernel, slots), out_shape=jax.Shape...]
    all_to_all x3 -> x0, starting transfers between devices: 39.4 us -> none  [the longest x1 15.3 us: on_device(): lax.all_to_all(result.astype(jnp.bfloat16), 'sn', split_axis=0, concat_ax...]
    all_gather x1, blocking collectives: 11.1 us -> 44 us  [tables(): meta = lax.all_gather(meta, 'sn').reshape(NZ, NXC, count, -1)]
    all_gather x1 -> x0, waiting for transfers between devices: 30.6 us -> none  [on_device(): full_panel = lax.all_gather(panel_blocks, 'br', axis=1, tiled=True)]
    dot_general x4 -> x1, matrix products: 19.3 us -> 0.43 us  [on_device(): jnp.einsum('cba,cbd->cad', panel_blocks, column, preferred_element_type=F32)]
    gather x2 -> x7, local copies, waits for them, and re-layouts: 18.2 us -> 3.88 us  [the longest x4 2.22 us: column_of(): return lax.dynamic_index_in_dim(values, xc, 1, keepdims=False)[sources]]
    scatter x2 -> x0, local copies, waits for them, and re-layouts: 9.89 us -> none  [place_slots(): empty.at[slot_place].set(values)]
  transfers between devices with their start and end apart: 5 -> 1, of which waited for: 4 -> 1; matrix products, arithmetic and copies ran while one was open for 8% -> 0% of each run, Pallas kernels for 0% -> 0%
where the time goes in v1:
time: 281 us
  Pallas kernels  172 us (61%)
  blocking collectives  44 us (16%)
  waiting for transfers between devices  31.3 us (11%)
  between operations  15 us (5%)
  local copies, waits for them, and re-layouts  11.5 us (4%)
  other arithmetic  6.45 us (2%)
    pallas_call x1, Pallas kernels, send_children(): pl.pallas_call(functools.partial(send_kernel, slots), out_shape=jax.Shape...  78.6 us
    pallas_call x1, Pallas kernels, return_children(): pl.pallas_call(functools.partial(return_kernel, slots), out_shape=jax.Sha...  74 us
    all_gather x1, blocking collectives, tables(): meta = lax.all_gather(meta, 'sn').reshape(NZ, NXC, count, -1)  44 us
    reduce_scatter x1, waiting for transfers between devices, on_device(): summed = lax.psum_scatter(term, 'br', scatter_dimension=1, tiled=True)  31.3 us
    pallas_call x1, Pallas kernels, parent_step(): pl.pallas_call(parent_kernel, out_shape=(jax.ShapeDtypeStruct((ancestors...  19.4 us
  transfers between devices with their start and end apart: 1, of which 1 were waited for; matrix products, arithmetic and copies ran while one was open for 0% of the time, Pallas kernels for 0%

profile of v1, /device:TPU:1, one launch (start us, length us, event | category | flops | bytes accessed | tf_op | source)
XLA Modules:
  0.0 280.8 jit_solution(9898689468711512711)
XLA Ops:
  7.2 0.7 pad_add_fusion
  8.1 44.0 %all-gather = s32[64,1,120]{2,1,0:T(1,128)S(1)} all-gather(s32[1,1,120]{2,1,0:T(1,128)S(1)} %reshape.238), channel_id=1, replica_groups=mesh['sn'=64,'br'=4] {'sn'}, dimensions={0}, use_global_device_ids=true | all-gather | bytes 31200 | tf_op jit(solution)/shard_map/all_gather | solution.py:319
  53.1 2.8 convert_reduce_fusion
  55.9 0.5 gather_fusion.1
  56.5 0.6 gather_fusion.2
  57.0 0.6 gather_fusion
  57.6 0.4 select_reduce_fusion.4
  58.1 0.6 reduce_max.9
  59.4 0.6 gather_fusion.6
  60.0 0.6 gather_fusion.5
  60.5 0.6 gather_fusion.4
  61.1 0.6 gather_fusion.3
  62.1 78.6 %conditional.2 = (bf16[2,8,4,2,128,128]{5,4,3,2,1,0:T(8,128)(2,1)}) conditional(s32[]{:T(128)} %convert_element_type.18, (s32[8,16]{1,0:T(8,128)S(1)}, s32[8,16]{1,0:T(8,128)S(1)}, bf16[24,128,128]{2,1,0:T(8,128)(2,1)}) %tuple.20, (s32[8,16]{1,0:T(8,128)S(1)}, s32[8,16]{1,0:T(8,128)S(1)}, bf16[24,128,128]{2,1,0:T(8,128)(2,1)}) %tuple.20), branch_computations={%region_6.7_spmd, %region_7.8_spmd} | conditional | bytes 8 | solution.py:371
  62.2 78.6 %branch_1_fun.2 = bf16[2,8,4,2,128,128]{5,4,3,2,1,0:T(8,128)(2,1)} custom-call(s32[8,16]{1,0:T(8,128)S(1)} %get-tuple-element.77.z_child, s32[8,16]{1,0:T(8,128)S(1)} %get-tuple-element.78.x_pick, bf16[24,128,128]{2,1,0:T(8,128)(2,1)} %get-tuple-element.79.panel), custom_call_target="tpu_custom_call" | custom-call | tf_op jit(solution)/shard_map/cond/branch_1_fun/pallas_call | solution.py:123
  140.8 3.4 %copy-done = bf16[1,16,16,128,128]{4,3,2,1,0:T(8,128)(2,1)S(1)} copy-done((bf16[1,16,16,128,128]{4,3,2,1,0:T(8,128)(2,1)S(1)}, bf16[1,16,16,128,128]{4,3,2,1,0:T(8,128)(2,1)}, u32[]{:S(2)}) %copy-start) | copy-done | bytes 8388632
  144.1 19.4 %shard_map.102 = (bf16[4,128,128]{2,1,0:T(8,128)(2,1)}, bf16[32,128]{1,0:T(8,128)(2,1)}, bf16[2,8,4,2,128,128]{5,4,3,2,1,0:T(8,128)(2,1)S(1)}) custom-call(s32[32,4]{1,0:T(8,128)S(1)} %bitcast.36, bf16[16,16,128,128]{3,2,1,0:T(8,128)(2,1)S(1)} %bitcast.34, bf16[16,128,128]{2,1,0:T(8,128)(2,1)S(1)} %bitcast.35, bf16[128,128]{1,0:T(8,128)(2,1)S(1)} %bitcast.37, ...), custom_call_target="tpu_custom_call" | custom-call | tf_op jit(solution)/shard_map/pallas_call | solution.py:292
  163.6 74.3 %conditional.3 = (bf16[24,128,128]{2,1,0:T(8,128)(2,1)S(1)}) conditional(s32[]{:T(128)} %convert_element_type.18, (pred[8,24]{1,0:T(8,128)(4,1)S(1)}, s32[8,24]{1,0:T(8,128)S(1)}, s32[8,16,24]{2,1,0:T(8,128)S(1)}, s32[8,16,24]{2,1,0:T(8,128)S(1)}, s32[8,16,24]{2,1,0:T(8,128)S(1)}, /*index=5*/s32[24]{0:T(128)S(1)}, pred[24]{0:T(512)(128)(4,1)S(1)}, ...), branch_computations={%region_8.10_spmd, %region_10.12_spmd} | conditional | flops 12256 | bytes 38656 | solution.py:380
  163.9 74.0 %branch_1_fun.3 = bf16[24,128,128]{2,1,0:T(8,128)(2,1)S(1)} custom-call(s32[8,16]{1,0:T(8,128)S(1)} %select_reduce_fusion.1.z_pick, s32[24]{0:T(128)S(1)} %fusion.3.child_slot, bf16[2,8,4,2,128,128]{5,4,3,2,1,0:T(8,128)(2,1)S(1)} %get-tuple-element.97.y), custom_call_target="tpu_custom_call" | custom-call | tf_op jit(solution)/shard_map/cond/branch_1_fun/pallas_call | solution.py:225
  238.0 0.4 convolution_bitcast_fusion
  238.4 1.6 copy.54
  240.1 31.3 %reduce-scatter.2.cloned.1.call-done = f32[24,32,128]{2,0,1:T(8,128)} async-done(((f32[24,128,128]{2,0,1:T(8,128)}), f32[24,32,128]{2,0,1:T(8,128)}) %reduce-scatter.2.cloned.1.call-update) | async-done | bytes 393232 | tf_op jit(solution)/shard_map/reduce_scatter | solution.py:390
  271.3 1.1 subtract_convert_fusion
  272.4 0.7 copy.55
  273.1 0.9 copy.65
  (49 shorter events, 2.0 us)
Async XLA Ops:
  7.2 264.2 %reduce-scatter.2.cloned.1.call-start = ((), (), s32[]{:S(2)}) async-start(), calls=%async_computation.1 | async-start | bytes 1966080 | tf_op jit(solution)/shard_map/reduce_scatter | solution.py:390
  62.1 78.6 %copy-start.1 = (bf16[1,2048,128]{2,1,0:T(8,128)(2,1)S(1)}, bf16[1,2048,128]{2,1,0:T(8,128)(2,1)}, u32[]{:S(2)}) copy-start(bf16[1,2048,128]{2,1,0:T(8,128)(2,1)} %param.12) | copy-start | bytes 1572868
  62.1 78.6 %copy-start.2 = (bf16[1,128,128]{2,1,0:T(8,128)(2,1)S(1)}, bf16[1,128,128]{2,1,0:T(8,128)(2,1)}, u32[]{:S(2)}) copy-start(bf16[1,128,128]{2,1,0:T(8,128)(2,1)} %param.13) | copy-start | bytes 98308
  140.8 3.4 %copy-start = (bf16[1,16,16,128,128]{4,3,2,1,0:T(8,128)(2,1)S(1)}, bf16[1,16,16,128,128]{4,3,2,1,0:T(8,128)(2,1)}, u32[]{:S(2)}) copy-start(bf16[1,16,16,128,128]{4,3,2,1,0:T(8,128)(2,1)} %param.11) | copy-start | bytes 25165828
  163.6 74.3 %copy-start.3 = (bf16[24,128,128]{2,1,0:T(8,128)(2,1)S(1)}, bf16[24,128,128]{2,1,0:T(8,128)(2,1)}, u32[]{:S(2)}) copy-start(bf16[24,128,128]{2,1,0:T(8,128)(2,1)} %param.16) | copy-start | bytes 2359300
  237.9 33.4 %copy-start.4 = (bf16[24,32,128]{2,1,0:T(8,128)(2,1)S(1)}, bf16[24,32,128]{2,1,0:T(8,128)(2,1)}, u32[]{:S(2)}) copy-start(bf16[24,32,128]{2,1,0:T(8,128)(2,1)} %param.17) | copy-start | bytes 589828
Sparse Core Ops, SparseCore 0:
  240.2 31.1 reduce-scatter.1

commit v2 on v0

v2 whole, which is shorter than its diff:
```python
import functools

import jax
import jax.numpy as jnp
from jax import lax
from jax.experimental import pallas as pl
from jax.experimental.pallas import tpu as pltpu
from jax.sharding import PartitionSpec as P

NZ = 8
NXC = 8
NB = 4
CAP = 2
MESH = pl.DeviceIdType.MESH
BF16 = jnp.bfloat16
F32 = jnp.float32


STEPS = (0, 1, 7, 2, 6, 3, 5, 4)
HALVES = NZ // NB
PICKS = NXC * CAP
Z_CHILD = 0
X_PICK = Z_CHILD + NZ * PICKS
Z_PICK = X_PICK + NZ * PICKS
SPOTS = Z_PICK + NZ * PICKS
SLOT = SPOTS + NZ * PICKS * NB


def place():
    sn = lax.axis_index("sn")
    return lax.div(sn, NXC), lax.rem(sn, NXC), lax.axis_index("br")


def signal(sn, row):
    pl.semaphore_signal(
        pltpu.get_barrier_semaphore(), inc=1, device_id=(sn, row), device_id_type=MESH
    )


def routes_kernel(meta, out, send_sem, near_sem, far_sem):
    z, xc, k = place()

    def mate_z(d):
        return lax.rem(z + d, NZ) * NXC + xc

    def mate_xc(d):
        return z * NXC + lax.rem(xc + d, NXC)

    for d in range(1, NZ):
        signal(mate_z(d), k)
    for d in range(1, NXC):
        signal(mate_xc(d), k)
    pl.semaphore_wait(pltpu.get_barrier_semaphore(), NZ + NXC - 2)

    pltpu.make_async_copy(meta, out.at[xc, z], near_sem).start()
    for d in range(1, NZ):
        pltpu.make_async_remote_copy(
            src_ref=meta,
            dst_ref=out.at[xc, z],
            send_sem=send_sem.at[0],
            recv_sem=near_sem,
            device_id=(mate_z(d), k),
            device_id_type=MESH,
        ).start()
    pltpu.make_async_copy(out.at[xc], out.at[xc], near_sem).wait()
    for d in range(1, NXC):
        pltpu.make_async_remote_copy(
            src_ref=out.at[xc],
            dst_ref=out.at[xc],
            send_sem=send_sem.at[1],
            recv_sem=far_sem,
            device_id=(mate_xc(d), k),
            device_id_type=MESH,
        ).start()
    some = out.at[pl.ds(0, NXC - 1)]
    pltpu.make_async_copy(some, some, far_sem).wait()
    part = out.at[0, pl.ds(0, NZ - 1)]
    pltpu.make_async_copy(part, part, send_sem.at[0]).wait()
    pltpu.make_async_copy(some, some, send_sem.at[1]).wait()


def all_routes(meta):
    vmem = pl.BlockSpec(memory_space=pltpu.VMEM)
    return pl.pallas_call(
        routes_kernel,
        out_shape=jax.ShapeDtypeStruct((NXC, NZ) + meta.shape, meta.dtype),
        in_specs=[vmem],
        out_specs=vmem,
        scratch_shapes=[
            pltpu.SemaphoreType.DMA((2,)),
            pltpu.SemaphoreType.DMA,
            pltpu.SemaphoreType.DMA,
        ],
        compiler_params=pltpu.CompilerParams(collective_id=1, has_side_effects=True),
    )(meta)


def greet():
    z, xc, k = place()

    def along_z(d, carry):
        signal(lax.rem(z + d, NZ) * NXC + xc, k)
        return carry

    def in_plane(o, carry):
        signal(
            z * NXC + lax.rem(xc + lax.div(o, NB), NXC), lax.rem(k + lax.rem(o, NB), NB)
        )
        return carry

    lax.fori_loop(1, NZ, along_z, 0)
    lax.fori_loop(1, NXC * NB, in_plane, 0)
    pl.semaphore_wait(pltpu.get_barrier_semaphore(), NZ - 1 + NXC * NB - 1)


def whole_kernel(
    slots,
    table,
    panel,
    anc,
    parent_blocks,
    dinv,
    child_dinv,
    below_out,
    diag_out,
    column,
    child_diag,
    full,
    z_send,
    x_send,
    x,
    y,
    z_home,
    t_send,
    t_got,
    z_got,
    y_got,
    f_sem,
    zs_sem,
    zr_sem,
    xs_sem,
    xr_sem,
    ys_sem,
    yr_sem,
    hs_sem,
    hr_sem,
    ts_sem,
    tr_sem,
):
    z, xc, k = place()
    ancestors, width = parent_blocks.shape[0], parent_blocks.shape[-1]
    rows = width // NB
    count = column.shape[0]
    share = ancestors // NB
    plane = lax.rem(k - xc + 2 * NB, NB)

    def full_copy(i):
        return pltpu.make_async_copy(
            anc.at[i], full.at[i + 1, pl.ds(1, ancestors)], f_sem.at[i]
        )

    for i in range(ancestors):
        full_copy(i).start()
    greet()

    def ahead(n):
        return lax.rem(z + STEPS[n], NZ)

    def behind(n):
        return lax.rem(z + NZ - STEPS[n], NZ)

    def z_copy(n):
        return pltpu.make_async_remote_copy(
            src_ref=z_send.at[n],
            dst_ref=z_got[n],
            send_sem=zs_sem.at[n],
            recv_sem=zr_sem.at[n],
            device_id=(ahead(n) * NXC + xc, k),
            device_id_type=MESH,
        )

    for n in range(1, NZ):

        def fill(j, carry, n=n):
            z_send[n, j] = panel[table[Z_CHILD + ahead(n) * PICKS + j]]
            return carry

        lax.fori_loop(0, slots, fill, 0)
        z_copy(n).start()

    def own(j, carry):
        z_got[0][j] = panel[table[Z_CHILD + z * PICKS + j]]
        return carry

    lax.fori_loop(0, slots, own, 0)

    def forward(n):
        if n:
            z_copy(n).wait_recv()

        def step(o, carry):
            other = lax.rem(xc + o, NXC)
            target = lax.rem(other + n, NB)
            for rank in range(CAP):
                pick = table[X_PICK + behind(n) * PICKS + other * CAP + rank]
                x_send[n * NXC + other, rank] = z_got[n][pick]
            here = jnp.logical_and(o == 0, k == target)

            @pl.when(here)
            def _():
                pltpu.make_async_copy(
                    x_send.at[n * NXC + other], x.at[n // NB, xc, k], xr_sem.at[n // NB]
                ).start()

            @pl.when(jnp.logical_not(here))
            def _():
                pltpu.make_async_remote_copy(
                    src_ref=x_send.at[n * NXC + other],
                    dst_ref=x.at[n // NB, xc, k],
                    send_sem=xs_sem,
                    recv_sem=xr_sem.at[n // NB],
                    device_id=(z * NXC + other, target),
                    device_id_type=MESH,
                ).start()

            return carry

        lax.fori_loop(0, NXC, step, 0)

    def parent():
        diag = dinv[...].astype(F32)
        for i in range(ancestors):
            full_copy(i).wait()
            total = jnp.zeros((width, width), F32)
            for l in range(0, ancestors, NB):
                left = jnp.concatenate([full[i + 1, 1 + l + m] for m in range(NB)], axis=1)
                right = jnp.concatenate([parent_blocks[l + m] for m in range(NB)], axis=0)
                total += jnp.dot(left, right, preferred_element_type=F32)
            total = (-total).astype(BF16)
            full[i + 1, 0] = total
            full[0, i + 1] = total.T
            diag -= lax.dot_general(
                parent_blocks[i], total, (((0,), (0,)), ((), ())), preferred_element_type=F32
            )
        full[0, 0] = diag.astype(BF16)
        for i in range(share):
            below_out[i] = full[1 + k * share + i, 0]
        diag_out[...] = full[0, 0, pl.ds(k * rows, rows)]

    def children(half):
        step = jnp.int32(0)
        for p in range(NB):
            step = jnp.where(plane == p, STEPS[half * NB + p], step)
        source = lax.rem(z + NZ - step, NZ)
        pltpu.make_async_copy(x.at[half], x.at[half], xr_sem.at[half]).wait()

        def group(o, carry):
            other = lax.rem(xc + o, NXC)
            first = half * NXC * NB + other * NB
            for rank in range(CAP):
                base = SPOTS + ((source * NXC + other) * CAP + rank) * NB
                spot = [table[base + l] for l in range(NB)]
                right = jnp.concatenate([x[half, other, l, rank] for l in range(NB)], axis=0)
                for i in range(NB):
                    left = jnp.concatenate([full[spot[i], spot[l]] for l in range(NB)], axis=1)
                    product = jnp.dot(left, right, preferred_element_type=F32)
                    y[first + i, rank] = (-product).astype(BF16)
            for p in range(NB):
                landing = y_got[half * NB + p]
                arrived = yr_sem.at[half * NB + p]

                @pl.when(plane == p)
                def _(landing=landing, arrived=arrived):
                    def back(i, carry):
                        row = lax.rem(k + i, NB)
                        here = jnp.logical_and(o == 0, i == 0)

                        @pl.when(here)
                        def _():
                            pltpu.make_async_copy(
                                y.at[first + row], landing.at[pl.ds(xc * CAP, CAP)], arrived
                            ).start()

                        @pl.when(jnp.logical_not(here))
                        def _():
                            pltpu.make_async_remote_copy(
                                src_ref=y.at[first + row],
                                dst_ref=landing.at[pl.ds(xc * CAP, CAP)],
                                send_sem=ys_sem,
                                recv_sem=arrived,
                                device_id=(z * NXC + other, row),
                                device_id_type=MESH,
                            ).start()

                        return carry

                    lax.fori_loop(0, NB, back, 0)

            return carry

        lax.fori_loop(0, NXC, group, 0)

    def home_copy(n, zone):
        return pltpu.make_async_remote_copy(
            src_ref=z_send.at[n],
            dst_ref=z_home.at[pl.ds(zone * slots, slots)],
            send_sem=hs_sem.at[n],
            recv_sem=hr_sem.at[n],
            device_id=(behind(n) * NXC + xc, k),
            device_id_type=MESH,
        )

    def backward(n):
        pltpu.make_async_copy(y_got[n], y_got[n], yr_sem.at[n]).wait()
        if n:
            z_copy(n).wait_send()

        def pack(j, carry):
            block = y_got[n][table[Z_PICK + behind(n) * PICKS + j]]
            if n:
                z_send[n, j] = block
            else:
                z_home[z * slots + j] = block
            return carry

        lax.fori_loop(0, slots, pack, 0)
        if n:
            home_copy(n, z).start()

    parent()
    for n in range(NB):
        forward(n)
    children(0)
    for n in range(NB, NZ):
        forward(n)
    for n in range(NB):
        backward(n)
    children(1)
    for n in range(NB, NZ):
        backward(n)
    for n in range(1, NZ):
        home_copy(n, ahead(n)).wait_recv()

    batch = count // NB

    def term_copy(b, d):
        row = lax.rem(k + d, NB)
        return pltpu.make_async_remote_copy(
            src_ref=t_send.at[row, pl.ds(b * batch, batch)],
            dst_ref=t_got.at[k, pl.ds(b * batch, batch)],
            send_sem=ts_sem,
            recv_sem=tr_sem.at[b],
            device_id=(z * NXC + xc, row),
            device_id_type=MESH,
        )

    for b in range(NB):

        def unpack(i, carry):
            block = z_home[table[SLOT + i]]
            column[i] = block
            term = lax.dot_general(
                panel[i], block, (((0,), (0,)), ((), ())), preferred_element_type=F32
            )
            for q in range(NB):
                t_send[q, i] = term[q * rows : (q + 1) * rows]
            return carry

        lax.fori_loop(b * batch, (b + 1) * batch, unpack, 0)
        for d in range(1, NB):
            term_copy(b, d).start()

    for b in range(NB):
        got = t_got.at[pl.ds(0, NB - 1), pl.ds(b * batch, batch)]
        pltpu.make_async_copy(got, got, tr_sem.at[b]).wait()

        def finish(i, carry):
            total = t_send[k, i]
            for d in range(1, NB):
                total += t_got[lax.rem(k + d, NB), i]
            child_diag[i] = (child_dinv[i].astype(F32) - total).astype(BF16)
            return carry

        lax.fori_loop(b * batch, (b + 1) * batch, finish, 0)

    for n in range(1, NZ):
        home_copy(n, z).wait_send()
    remote = pl.ds(0, NZ * NXC - HALVES)
    pltpu.make_async_copy(x_send.at[remote], x_send.at[remote], xs_sem).wait()
    pltpu.make_async_copy(y.at[remote], y.at[remote], ys_sem).wait()
    sent = t_send.at[pl.ds(0, NB - 1)]
    pltpu.make_async_copy(sent, sent, ts_sem).wait()


def whole(slots, ident, table, panel_blocks, anc, parent_blocks, dinv, child_dinv):
    ancestors, width = parent_blocks.shape[0], parent_blocks.shape[-1]
    count, rows = panel_blocks.shape[0], width // NB
    block = (width, width)
    vmem = pl.BlockSpec(memory_space=pltpu.VMEM)
    dma = pltpu.SemaphoreType.DMA
    return pl.pallas_call(
        functools.partial(whole_kernel, slots),
        out_shape=(
            jax.ShapeDtypeStruct((ancestors // NB,) + block, BF16),
            jax.ShapeDtypeStruct((rows, width), BF16),
            jax.ShapeDtypeStruct((count,) + block, BF16),
            jax.ShapeDtypeStruct((count, rows, width), BF16),
        ),
        in_specs=[
            pl.BlockSpec(memory_space=pltpu.SMEM),
            vmem,
            pl.BlockSpec(memory_space=pl.ANY),
            vmem,
            vmem,
            vmem,
        ],
        out_specs=(vmem, vmem, vmem, vmem),
        scratch_shapes=[
            pltpu.VMEM((ancestors + 1, ancestors + 1) + block, BF16),
            pltpu.VMEM((NZ, slots) + block, BF16),
            pltpu.VMEM((NZ * NXC, CAP) + block, BF16),
            pltpu.VMEM((HALVES, NXC, NB, CAP) + block, BF16),
            pltpu.VMEM((HALVES * NXC * NB, CAP) + block, BF16),
            pltpu.VMEM((NZ * slots,) + block, BF16),
            pltpu.VMEM((NB, count, rows, width), F32),
            pltpu.VMEM((NB, count, rows, width), F32),
            [pltpu.VMEM((slots,) + block, BF16) for _ in range(NZ)],
            [pltpu.VMEM((PICKS,) + block, BF16) for _ in range(NZ)],
            dma((ancestors,)),
            dma((NZ,)),
            dma((NZ,)),
            dma,
            dma((HALVES,)),
            dma,
            dma((NZ,)),
            dma((NZ,)),
            dma((NZ,)),
            dma,
            dma((NB,)),
        ],
        compiler_params=pltpu.CompilerParams(
            collective_id=ident, has_side_effects=True, vmem_limit_bytes=56 * 2**20
        ),
    )(table, panel_blocks, anc, parent_blocks, dinv, child_dinv)


def tables(child_route, child_pattern):
    z, xc, _ = place()
    count = child_route.shape[0]
    meta = jnp.concatenate([child_route.reshape(-1), child_pattern.T.reshape(-1)])
    meta = jnp.pad(meta, (0, 8 * 128 - meta.shape[0])).reshape(8, 128)
    meta = all_routes(meta).reshape(NXC, NZ, -1)[..., : (1 + NB) * count]
    route = meta[..., :count]
    pattern = meta[..., count:].reshape(NXC, NZ, NB, count)
    goal = route // NXC
    earlier = jnp.arange(count)[None, :] < jnp.arange(count)[:, None]
    spot = jnp.sum(((goal[..., :, None] == goal[..., None, :]) & earlier).astype(jnp.int32), -1)
    rank = jnp.sum(((route[..., :, None] == route[..., None, :]) & earlier).astype(jnp.int32), -1)
    fullest = jnp.max(spot) + 1

    def of_xc(values):
        return lax.dynamic_index_in_dim(values, xc, 0, keepdims=False)

    places = jnp.arange(PICKS, dtype=jnp.int32)[:, None]
    route_xc, spot_xc, rank_xc = of_xc(route), of_xc(spot), of_xc(rank)
    goal_xc = route_xc // NXC
    own_goal = lax.dynamic_index_in_dim(goal_xc, z, 0, keepdims=False)
    own_spot = lax.dynamic_index_in_dim(spot_xc, z, 0, keepdims=False)
    hit = (own_goal == jnp.arange(NZ)[:, None, None]) & (own_spot == places)
    z_child = jnp.sum(jnp.where(hit, jnp.arange(count, dtype=jnp.int32), 0), -1)

    mine = (goal_xc == z)[:, None]
    target = ((route_xc % NXC) * CAP + rank_xc)[:, None]
    via = spot_xc[:, None]
    x_pick = jnp.sum(jnp.where(mine & (target == places), via, 0), -1)
    z_pick = jnp.sum(jnp.where(mine & (via == places), target, 0), -1)

    hit = (route == z * NXC + xc)[:, :, None] & (rank[:, :, None] == jnp.arange(CAP)[:, None])
    spots = jnp.sum(jnp.where(hit[:, :, :, None], pattern[:, :, None], 0), -1)
    spots = jnp.swapaxes(spots, 0, 1)

    def with_slots(slots):
        parts = (z_child, x_pick, z_pick, spots, own_goal * slots + own_spot)
        return jnp.concatenate([part.reshape(-1) for part in parts])

    return fullest, with_slots


def on_device(
    anc_inverse, parent_panel, parent_dinv, child_route, child_pattern, child_panel, child_dinv
):
    width = parent_dinv.shape[-1]
    ancestors = anc_inverse.shape[1]
    count = child_route.shape[0]
    few, most = NXC, PICKS
    fullest, with_slots = tables(child_route, child_pattern)
    fits = fullest <= few
    table = with_slots(jnp.where(fits, few, most))
    below, diag, column, child_diag = lax.cond(
        fits,
        functools.partial(whole, few, 2),
        functools.partial(whole, most, 3),
        table,
        child_panel.reshape(count, width, width),
        anc_inverse[0],
        parent_panel[0].reshape(ancestors, width, width),
        parent_dinv[0],
        child_dinv,
    )
    return (below.reshape(1, -1, width), diag[None], column, child_diag)


def solution(mesh):
    placed = (
        P("sn", None, None, None, None),
        P("sn", None, None),
        P("sn", None, None),
        P("sn", None),
        P("sn", None),
        P("sn", "br", None),
        P("sn", "br", None),
    )
    return jax.shard_map(
        on_device,
        mesh=mesh,
        in_specs=placed,
        out_specs=(
            P("sn", "br", None),
            P("sn", "br", None),
            P("sn", "br", None),
            P("sn", "br", None),
        ),
        check_vma=False,
    )
```

time: 611 us -> 221 us (0.36)
  waiting for transfers between devices: 476 us -> 0 us
  Pallas kernels: 0 us -> 207 us
  starting transfers between devices: 39.5 us -> 0 us
  local copies, waits for them, and re-layouts: 39.1 us -> 5.98 us
  matrix products: 19.3 us -> 0 us
  between operations: 14.2 us -> 1.47 us
  blocking collectives: 11.1 us -> 0 us
    all_to_all x3 -> x0, waiting for transfers between devices: 421 us -> none  [the longest x1 327 us: on_device(): lax.all_to_all(place_slots(full_panel), 'sn', split_axis=0, concat_axis=0...]
    pallas_call x0 -> x2, Pallas kernels: none -> 207 us  [the longest x1 188 us: whole(): pl.pallas_call(functools.partial(whole_kernel, slots), out_shape=(jax.Sha...]
    all_to_all x3 -> x0, starting transfers between devices: 39.4 us -> none  [the longest x1 15.3 us: on_device(): lax.all_to_all(result.astype(jnp.bfloat16), 'sn', split_axis=0, concat_ax...]
    all_gather x1 -> x0, waiting for transfers between devices: 30.6 us -> none  [on_device(): full_panel = lax.all_gather(panel_blocks, 'br', axis=1, tiled=True)]
    reduce_scatter x1 -> x0, waiting for transfers between devices: 23.5 us -> none  [on_device(): summed = lax.psum_scatter(diag_term, 'br', scatter_dimension=1, tiled=True)]
    dot_general x4 -> x0, matrix products: 19.3 us -> none  [the longest x1 15.1 us: on_device(): jnp.einsum('ncmkab,nckbd->ncmad', picked, lax.all_to_all(place_slots(full...]
    gather x2 -> x0, local copies, waits for them, and re-layouts: 18.2 us -> none  [the longest x1 14.5 us: on_device(): picked = full_inverse[row_pattern[..., :, None], pattern_buf[..., None, :]]]
    all_gather x1 -> x0, blocking collectives: 11.1 us -> none  [on_device(): below_col = lax.all_gather(own_below, 'br', axis=0, tiled=True)]
  transfers between devices with their start and end apart: 5 -> 0, of which waited for: 4 -> 0; matrix products, arithmetic and copies ran while one was open for 8% -> 0% of each run, Pallas kernels for 0% -> 0%
where the time goes in v2:
time: 221 us
  Pallas kernels  207 us (94%)
  other arithmetic  6.03 us (3%)
  local copies, waits for them, and re-layouts  5.98 us (3%)
    pallas_call x1, Pallas kernels, whole(): pl.pallas_call(functools.partial(whole_kernel, slots), out_shape=(jax.Sha...  188 us
    pallas_call x1, Pallas kernels, all_routes(): pl.pallas_call(routes_kernel, out_shape=jax.ShapeDtypeStruct((NXC, NZ) +...  19 us

profile of v2, /device:TPU:1, one launch (start us, length us, event | category | flops | bytes accessed | tf_op | source)
XLA Modules:
  0.0 221.1 jit_solution(14399771739327213060)
XLA Ops:
  0.7 0.8 reshape.170
  1.4 0.7 pad_add_fusion
  2.2 0.6 pad_bitcast_fusion.meta
  2.8 19.0 %shard_map.112 = s32[8,8,8,128]{3,2,1,0:T(8,128)} custom-call(s32[8,128]{1,0:T(8,128)} %pad_bitcast_fusion.meta), custom_call_target="tpu_custom_call" | custom-call | tf_op jit(solution)/shard_map/pallas_call | solution.py:84
  21.8 1.0 reshape.172
  22.8 0.1 slice.12
  23.0 2.8 %convert_reduce_fusion = (s32[8,8,24]{2,1,0:T(8,128)S(1)}, s32[8,8,24]{2,1,0:T(8,128)S(1)}) fusion(s32[8,8,24]{2,1,0:T(8,128)S(1)} %get-tuple-element.112, pred[24,24]{1,0:T(8,128)(4,1)S(1)} %iota_compare_fusion.3, s32[8,8,24]{2,1,0:T(8,128)S(1)} %get-tuple-element.111), kind=kLoop, calls=%fused_computation | loop fusion | flops 291840 | bytes 25152 | tf_op jit(solution)/shard_map/reduce_sum | solution.py:458
  25.8 0.6 reduce_max.9
  27.1 0.2 select_reduce_fusion.3
  27.4 0.1 reshape.173
  27.5 0.3 select_reduce_fusion.1
  27.8 0.1 reshape.175
  27.9 0.1 reshape.174
  28.0 0.1 broadcast_in_dim.76
  28.1 1.2 select_reduce_fusion
  29.3 0.2 copy.22
  29.5 0.1 reshape.176
  29.7 188.6 %conditional.1 = ((bf16[4,128,128]{2,1,0:T(8,128)(2,1)S(1)}, bf16[32,128]{1,0:T(8,128)(2,1)S(1)}, bf16[24,128,128]{2,1,0:T(8,128)(2,1)S(1)}, bf16[24,32,128]{2,1,0:T(8,128)(2,1)S(1)})) conditional(s32[]{:T(128)} %convert_element_type.10, (bf16[1,16,16,128,128]{4,3,2,1,0:T(8,128)(2,1)}, bf16[1,2048,128]{2,1,0:T(8,128)(2,1)}, ...), branch_computations={%region_7.8_spmd, %region_8.9_spmd} | conditional | bytes 8 | solution.py:499
  29.9 188.4 %branch_1_fun.1 = (bf16[4,128,128]{2,1,0:T(8,128)(2,1)S(1)}, bf16[32,128]{1,0:T(8,128)(2,1)S(1)}, bf16[24,128,128]{2,1,0:T(8,128)(2,1)S(1)}, bf16[24,32,128]{2,1,0:T(8,128)(2,1)S(1)}) custom-call(s32[920]{0:T(1024)S(1)} %get-tuple-element.51.table, bf16[24,128,128]{2,1,0:T(8,128)(2,1)} %get-tuple-element.96.panel, bf16[16,16,128,128]{3,2,1,0:T(8,128)(2,1)} %bitcast.52, ...), custom_call_target="tpu_custom_call" | custom-call | tf_op jit(solution)/shard_map/cond/branch_1_fun/pallas_call | solution.py:401
  218.3 0.7 copy.40
  218.9 0.6 copy.41
  219.5 0.9 copy.42
  220.4 0.7 copy.43
  (18 shorter events, 0.2 us)

commit v3 on v2

--- a/solution.py
+++ b/solution.py
@@ -8,7 +8,9 @@
 from jax.sharding import PartitionSpec as P
 
 NZ = 8
-NXC = 8
+NX = 4
+CORES = 2
+NXC = NX * CORES
 NB = 4
 CAP = 2
 MESH = pl.DeviceIdType.MESH
@@ -16,14 +18,17 @@
 F32 = jnp.float32
 
 
-STEPS = (0, 1, 7, 2, 6, 3, 5, 4)
-HALVES = NZ // NB
+STEPS = (0, 4, 2, 6, 1, 7, 3, 5)
+AT_ONCE = 3
 PICKS = NXC * CAP
+PAIR = CORES * CAP
+SIZES = ((6, 3), (7, 3), (8, 3), (PICKS, PAIR))
 Z_CHILD = 0
 X_PICK = Z_CHILD + NZ * PICKS
 Z_PICK = X_PICK + NZ * PICKS
 SPOTS = Z_PICK + NZ * PICKS
-SLOT = SPOTS + NZ * PICKS * NB
+SPOT = 1 + NB
+SLOT = SPOTS + NXC * PAIR * SPOT
 
 
 def place():
@@ -115,6 +120,7 @@
 
 def whole_kernel(
     slots,
+    lanes,
     table,
     panel,
     anc,
@@ -129,13 +135,14 @@
     z_send,
     x_send,
     x,
-    y,
     z_home,
     t_send,
     t_got,
     z_got,
     y_got,
     f_sem,
+    fs_sem,
+    fr_sem,
     zs_sem,
     zr_sem,
     xs_sem,
@@ -152,11 +159,12 @@
     rows = width // NB
     count = column.shape[0]
     share = ancestors // NB
-    plane = lax.rem(k - xc + 2 * NB, NB)
+    cx, core = lax.div(xc, CORES), lax.rem(xc, CORES)
+    plane = lax.rem(k - cx + NB, NB)
 
     def full_copy(i):
         return pltpu.make_async_copy(
-            anc.at[i], full.at[i + 1, pl.ds(1, ancestors)], f_sem.at[i]
+            anc.at[i], full.at[0, i + 1, pl.ds(1, ancestors)], f_sem.at[i]
         )
 
     for i in range(ancestors):
@@ -179,14 +187,16 @@
             device_id_type=MESH,
         )
 
-    for n in range(1, NZ):
-
-        def fill(j, carry, n=n):
+    def launch(n):
+        def fill(j, carry):
             z_send[n, j] = panel[table[Z_CHILD + ahead(n) * PICKS + j]]
             return carry
 
         lax.fori_loop(0, slots, fill, 0)
         z_copy(n).start()
+
+    for n in range(1, 1 + AT_ONCE):
+        launch(n)
 
     def own(j, carry):
         z_got[0][j] = panel[table[Z_CHILD + z * PICKS + j]]
@@ -199,33 +209,42 @@
             z_copy(n).wait_recv()
 
         def step(o, carry):
-            other = lax.rem(xc + o, NXC)
-            target = lax.rem(other + n, NB)
-            for rank in range(CAP):
-                pick = table[X_PICK + behind(n) * PICKS + other * CAP + rank]
-                x_send[n * NXC + other, rank] = z_got[n][pick]
-            here = jnp.logical_and(o == 0, k == target)
+            other = lax.rem(cx + o, NX)
+            row = lax.rem(other + n, NB)
+            for lane in range(lanes):
+                pick = table[X_PICK + behind(n) * PICKS + other * PAIR + lane]
+                x_send[n * NX + other, lane] = z_got[n][pick]
+            here = jnp.logical_and(o == 0, jnp.logical_and(core == n // NB, k == row))
 
             @pl.when(here)
             def _():
                 pltpu.make_async_copy(
-                    x_send.at[n * NXC + other], x.at[n // NB, xc, k], xr_sem.at[n // NB]
+                    x_send.at[n * NX + other], x.at[xc, k], xr_sem.at[xc]
                 ).start()
 
             @pl.when(jnp.logical_not(here))
             def _():
                 pltpu.make_async_remote_copy(
-                    src_ref=x_send.at[n * NXC + other],
-                    dst_ref=x.at[n // NB, xc, k],
+                    src_ref=x_send.at[n * NX + other],
+                    dst_ref=x.at[xc, k],
                     send_sem=xs_sem,
-                    recv_sem=xr_sem.at[n // NB],
-                    device_id=(z * NXC + other, target),
+                    recv_sem=xr_sem.at[xc],
+                    device_id=(z * NXC + other * CORES + n // NB, row),
                     device_id_type=MESH,
                 ).start()
 
             return carry
 
-        lax.fori_loop(0, NXC, step, 0)
+        lax.fori_loop(0, NX, step, 0)
+
+    sibling = pltpu.make_async_remote_copy(
+        src_ref=full.at[0],
+        dst_ref=full.at[1],
+        send_sem=fs_sem,
+        recv_sem=fr_sem,
+        device_id=(z * NXC + cx * CORES + 1 - core, k),
+        device_id_type=MESH,
+    )
 
     def parent():
         diag = dinv[...].astype(F32)
@@ -233,69 +252,62 @@
             full_copy(i).wait()
             total = jnp.zeros((width, width), F32)
             for l in range(0, ancestors, NB):
-                left = jnp.concatenate([full[i + 1, 1 + l + m] for m in range(NB)], axis=1)
+                left = jnp.concatenate([full[0, i + 1, 1 + l + m] for m in range(NB)], axis=1)
                 right = jnp.concatenate([parent_blocks[l + m] for m in range(NB)], axis=0)
                 total += jnp.dot(left, right, preferred_element_type=F32)
             total = (-total).astype(BF16)
-            full[i + 1, 0] = total
-            full[0, i + 1] = total.T
+            full[0, i + 1, 0] = total
+            full[0, 0, i + 1] = total.T
             diag -= lax.dot_general(
                 parent_blocks[i], total, (((0,), (0,)), ((), ())), preferred_element_type=F32
             )
-        full[0, 0] = diag.astype(BF16)
+        full[0, 0, 0] = diag.astype(BF16)
+        sibling.start()
         for i in range(share):
-            below_out[i] = full[1 + k * share + i, 0]
-        diag_out[...] = full[0, 0, pl.ds(k * rows, rows)]
+            below_out[i] = full[0, 1 + k * share + i, 0]
+        diag_out[...] = full[0, 0, 0, pl.ds(k * rows, rows)]
 
     def children(half):
-        step = jnp.int32(0)
-        for p in range(NB):
-            step = jnp.where(plane == p, STEPS[half * NB + p], step)
-        source = lax.rem(z + NZ - step, NZ)
-        pltpu.make_async_copy(x.at[half], x.at[half], xr_sem.at[half]).wait()
+        landing = y_got[half].at[pl.ds((plane * NX + cx) * lanes, lanes)]
+        sibling.wait_recv()
 
         def group(o, carry):
             other = lax.rem(xc + o, NXC)
-            first = half * NXC * NB + other * NB
-            for rank in range(CAP):
-                base = SPOTS + ((source * NXC + other) * CAP + rank) * NB
-                spot = [table[base + l] for l in range(NB)]
-                right = jnp.concatenate([x[half, other, l, rank] for l in range(NB)], axis=0)
+            pltpu.make_async_copy(x.at[other], x.at[other], xr_sem.at[other]).wait()
+            for lane in range(lanes):
+                base = SPOTS + (other * PAIR + lane) * SPOT
+                which = table[base]
+                spot = [table[base + 1 + l] for l in range(NB)]
+                right = jnp.concatenate([x[other, l, lane] for l in range(NB)], axis=0)
                 for i in range(NB):
-                    left = jnp.concatenate([full[spot[i], spot[l]] for l in range(NB)], axis=1)
+                    left = jnp.concatenate(
+                        [full[which, spot[i], spot[l]] for l in range(NB)], axis=1
+                    )
                     product = jnp.dot(left, right, preferred_element_type=F32)
-                    y[first + i, rank] = (-product).astype(BF16)
-            for p in range(NB):
-                landing = y_got[half * NB + p]
-                arrived = yr_sem.at[half * NB + p]
-
-                @pl.when(plane == p)
-                def _(landing=landing, arrived=arrived):
-                    def back(i, carry):
-                        row = lax.rem(k + i, NB)
-                        here = jnp.logical_and(o == 0, i == 0)
-
-                        @pl.when(here)
-                        def _():
-                            pltpu.make_async_copy(
-                                y.at[first + row], landing.at[pl.ds(xc * CAP, CAP)], arrived
-                            ).start()
-
-                        @pl.when(jnp.logical_not(here))
-                        def _():
-                            pltpu.make_async_remote_copy(
-                                src_ref=y.at[first + row],
-                                dst_ref=landing.at[pl.ds(xc * CAP, CAP)],
-                                send_sem=ys_sem,
-                                recv_sem=arrived,
-                                device_id=(z * NXC + other, row),
-                                device_id_type=MESH,
-                            ).start()
-
-                        return carry
-
-                    lax.fori_loop(0, NB, back, 0)
-
+                    x[other, i, lane] = (-product).astype(BF16)
+
+            def back(i, carry):
+                row = lax.rem(k + i, NB)
+                here = jnp.logical_and(o == 0, i == 0)
+
+                @pl.when(here)
+                def _():
+                    pltpu.make_async_copy(x.at[other, row], landing, yr_sem.at[half]).start()
+
+                @pl.when(jnp.logical_not(here))
+                def _():
+                    pltpu.make_async_remote_copy(
+                        src_ref=x.at[other, row],
+                        dst_ref=landing,
+                        send_sem=ys_sem,
+                        recv_sem=yr_sem.at[half],
+                        device_id=(z * NXC + other, row),
+                        device_id_type=MESH,
+                    ).start()
+
+                return carry
+
+            lax.fori_loop(0, NB, back, 0)
             return carry
 
         lax.fori_loop(0, NXC, group, 0)
@@ -311,12 +323,14 @@
         )
 
     def backward(n):
-        pltpu.make_async_copy(y_got[n], y_got[n], yr_sem.at[n]).wait()
+        half, first = n // NB, n % NB * NX * lanes
+        if n % NB == 0:
+            pltpu.make_async_copy(y_got[half], y_got[half], yr_sem.at[half]).wait()
         if n:
             z_copy(n).wait_send()
 
         def pack(j, carry):
-            block = y_got[n][table[Z_PICK + behind(n) * PICKS + j]]
+            block = y_got[half][first + table[Z_PICK + behind(n) * PICKS + j]]
             if n:
                 z_send[n, j] = block
             else:
@@ -327,16 +341,25 @@
         if n:
             home_copy(n, z).start()
 
+    forward(0)
     parent()
-    for n in range(NB):
+    for n in range(1, NB):
         forward(n)
-    children(0)
+        launch(n + AT_ONCE)
+    launch(NZ - 1)
+
+    @pl.when(core == 0)
+    def _():
+        children(0)
+
     for n in range(NB, NZ):
         forward(n)
-    for n in range(NB):
-        backward(n)
-    children(1)
-    for n in range(NB, NZ):
+
+    @pl.when(core == 1)
+    def _():
+        children(1)
+
+    for n in range(NZ):
         backward(n)
     for n in range(1, NZ):
         home_copy(n, ahead(n)).wait_recv()
@@ -385,21 +408,22 @@
 
     for n in range(1, NZ):
         home_copy(n, z).wait_send()
-    remote = pl.ds(0, NZ * NXC - HALVES)
+    remote = pl.ds(0, NZ * NX - 1)
     pltpu.make_async_copy(x_send.at[remote], x_send.at[remote], xs_sem).wait()
-    pltpu.make_async_copy(y.at[remote], y.at[remote], ys_sem).wait()
+    pltpu.make_async_copy(x_send.at[remote], x_send.at[remote], ys_sem).wait()
+    sibling.wait_send()
     sent = t_send.at[pl.ds(0, NB - 1)]
     pltpu.make_async_copy(sent, sent, ts_sem).wait()
 
 
-def whole(slots, ident, table, panel_blocks, anc, parent_blocks, dinv, child_dinv):
+def whole(slots, lanes, ident, table, panel_blocks, anc, parent_blocks, dinv, child_dinv):
     ancestors, width = parent_blocks.shape[0], parent_blocks.shape[-1]
     count, rows = panel_blocks.shape[0], width // NB
     block = (width, width)
     vmem = pl.BlockSpec(memory_space=pltpu.VMEM)
     dma = pltpu.SemaphoreType.DMA
     return pl.pallas_call(
-        functools.partial(whole_kernel, slots),
+        functools.partial(whole_kernel, slots, lanes),
         out_shape=(
             jax.ShapeDtypeStruct((ancestors // NB,) + block, BF16),
             jax.ShapeDtypeStruct((rows, width), BF16),
@@ -416,23 +440,24 @@
         ],
         out_specs=(vmem, vmem, vmem, vmem),
         scratch_shapes=[
-            pltpu.VMEM((ancestors + 1, ancestors + 1) + block, BF16),
+            pltpu.VMEM((CORES, ancestors + 1, ancestors + 1) + block, BF16),
             pltpu.VMEM((NZ, slots) + block, BF16),
-            pltpu.VMEM((NZ * NXC, CAP) + block, BF16),
-            pltpu.VMEM((HALVES, NXC, NB, CAP) + block, BF16),
-            pltpu.VMEM((HALVES * NXC * NB, CAP) + block, BF16),
+            pltpu.VMEM((NZ * NX, lanes) + block, BF16),
+            pltpu.VMEM((NXC, NB, lanes) + block, BF16),
             pltpu.VMEM((NZ * slots,) + block, BF16),
             pltpu.VMEM((NB, count, rows, width), F32),
             pltpu.VMEM((NB, count, rows, width), F32),
             [pltpu.VMEM((slots,) + block, BF16) for _ in range(NZ)],
-            [pltpu.VMEM((PICKS,) + block, BF16) for _ in range(NZ)],
+            [pltpu.VMEM((NB * NX * lanes,) + block, BF16) for _ in range(CORES)],
             dma((ancestors,)),
+            dma,
+            dma,
             dma((NZ,)),
             dma((NZ,)),
             dma,
-            dma((HALVES,)),
+            dma((NXC,)),
             dma,
-            dma((NZ,)),
+            dma((CORES,)),
             dma((NZ,)),
             dma((NZ,)),
             dma,
@@ -445,7 +470,8 @@
 
 
 def tables(child_route, child_pattern):
-    z, xc, _ = place()
+    z, xc, k = place()
+    cx, core = lax.div(xc, CORES), lax.rem(xc, CORES)
     count = child_route.shape[0]
     meta = jnp.concatenate([child_route.reshape(-1), child_pattern.T.reshape(-1)])
     meta = jnp.pad(meta, (0, 8 * 128 - meta.shape[0])).reshape(8, 128)
@@ -455,8 +481,9 @@
     goal = route // NXC
     earlier = jnp.arange(count)[None, :] < jnp.arange(count)[:, None]
     spot = jnp.sum(((goal[..., :, None] == goal[..., None, :]) & earlier).astype(jnp.int32), -1)
-    rank = jnp.sum(((route[..., :, None] == route[..., None, :]) & earlier).astype(jnp.int32), -1)
-    fullest = jnp.max(spot) + 1
+    chip = route // CORES
+    rank = jnp.sum(((chip[..., :, None] == chip[..., None, :]) & earlier).astype(jnp.int32), -1)
+    fullest, widest = jnp.max(spot) + 1, jnp.max(rank) + 1
 
     def of_xc(values):
         return lax.dynamic_index_in_dim(values, xc, 0, keepdims=False)
@@ -470,20 +497,30 @@
     z_child = jnp.sum(jnp.where(hit, jnp.arange(count, dtype=jnp.int32), 0), -1)
 
     mine = (goal_xc == z)[:, None]
-    target = ((route_xc % NXC) * CAP + rank_xc)[:, None]
+    lane_xc = rank_xc[:, None]
+    chip_xc = (route_xc // CORES % NX)[:, None]
     via = spot_xc[:, None]
-    x_pick = jnp.sum(jnp.where(mine & (target == places), via, 0), -1)
-    z_pick = jnp.sum(jnp.where(mine & (via == places), target, 0), -1)
-
-    hit = (route == z * NXC + xc)[:, :, None] & (rank[:, :, None] == jnp.arange(CAP)[:, None])
-    spots = jnp.sum(jnp.where(hit[:, :, :, None], pattern[:, :, None], 0), -1)
-    spots = jnp.swapaxes(spots, 0, 1)
-
-    def with_slots(slots):
+    x_pick = jnp.sum(jnp.where(mine & (chip_xc * PAIR + lane_xc == places), via, 0), -1)
+
+    turn = core * NB + lax.rem(k - cx + NB, NB)
+    step = jnp.sum(jnp.where(jnp.arange(NZ) == turn, jnp.array(STEPS, jnp.int32), 0))
+    source = lax.rem(z - step + NZ, NZ)
+
+    def of_source(values):
+        return lax.dynamic_index_in_dim(values, source, 1, keepdims=False)
+
+    there, lane = of_source(route), of_source(rank)
+    hit = (there // CORES == z * NX + cx)[:, None] & (lane[:, None] == jnp.arange(PAIR)[:, None])
+    which = (there % CORES != core).astype(jnp.int32)
+    spots = jnp.concatenate([which[:, None], of_source(pattern)], axis=1)
+    spots = jnp.sum(jnp.where(hit[:, :, None], spots[:, None], 0), -1)
+
+    def with_slots(slots, lanes):
+        z_pick = jnp.sum(jnp.where(mine & (via == places), chip_xc * lanes + lane_xc, 0), -1)
         parts = (z_child, x_pick, z_pick, spots, own_goal * slots + own_spot)
         return jnp.concatenate([part.reshape(-1) for part in parts])
 
-    return fullest, with_slots
+    return fullest, widest, with_slots
 
 
 def on_device(
@@ -492,15 +529,17 @@
     width = parent_dinv.shape[-1]
     ancestors = anc_inverse.shape[1]
     count = child_route.shape[0]
-    few, most = NXC, PICKS
-    fullest, with_slots = tables(child_route, child_pattern)
-    fits = fullest <= few
-    table = with_slots(jnp.where(fits, few, most))
-    below, diag, column, child_diag = lax.cond(
-        fits,
-        functools.partial(whole, few, 2),
-        functools.partial(whole, most, 3),
-        table,
+    fullest, widest, with_slots = tables(child_route, child_pattern)
+    fits = [(fullest <= slots) & (widest <= lanes) for slots, lanes in SIZES[:-1]]
+    size = jnp.int32(len(SIZES) - 1)
+    for i in reversed(range(len(fits))):
+        size = jnp.where(fits[i], i, size)
+    slots = sum(jnp.where(size == i, SIZES[i][0], 0) for i in range(len(SIZES)))
+    lanes = sum(jnp.where(size == i, SIZES[i][1], 0) for i in range(len(SIZES)))
+    below, diag, column, child_diag = lax.switch(
+        size,
+        [functools.partial(whole, *SIZES[i], 2 + i) for i in range(len(SIZES))],
+        with_slots(slots, lanes),
         child_panel.reshape(count, width, width),
         anc_inverse[0],
         parent_panel[0].reshape(ancestors, width, width),

time: 221 us -> 200 us (0.905)
  Pallas kernels: 207 us -> 184 us
    pallas_call x1, Pallas kernels: 188 us -> 165 us  [whole(): pl.pallas_call(functools.partial(whole_kernel, slots, lanes), out_shape=(...]
    reduce_sum x3 -> x4, other arithmetic: 4.31 us -> 4.84 us  [the longest x1 2.78 us: tables(): jnp.sum(((chip[..., :, None] == chip[..., None, :]) & earlier).astype(jnp...]
where the time goes in v3:
time: 200 us
  Pallas kernels  184 us (92%)
  other arithmetic  7.23 us (4%)
  local copies, waits for them, and re-layouts  5.98 us (3%)
  between operations  2.88 us (1%)
    pallas_call x1, Pallas kernels, whole(): pl.pallas_call(functools.partial(whole_kernel, slots, lanes), out_shape=(...  165 us
    pallas_call x1, Pallas kernels, all_routes(): pl.pallas_call(routes_kernel, out_shape=jax.ShapeDtypeStruct((NXC, NZ) +...  19 us

profile of v3, /device:TPU:1, one launch (start us, length us, event | category | flops | bytes accessed | tf_op | source)
XLA Modules:
  0.0 200.0 jit_solution(9193034986737812220)
XLA Ops:
  0.7 1.3 fusion.18
  2.6 0.8 reshape.204
  3.4 0.7 pad_add_fusion.1
  4.1 0.6 pad_bitcast_fusion.meta
  4.7 19.0 %shard_map.131 = s32[8,8,8,128]{3,2,1,0:T(8,128)} custom-call(s32[8,128]{1,0:T(8,128)} %pad_bitcast_fusion.meta), custom_call_target="tpu_custom_call" | custom-call | tf_op jit(solution)/shard_map/pallas_call | solution.py:89
  23.8 1.0 reshape.206
  25.0 2.8 %convert_reduce_fusion = (s32[8,8,24]{2,1,0:T(8,128)S(1)}, s32[8,8,24]{2,1,0:T(8,128)S(1)}) fusion(s32[8,8,24]{2,1,0:T(8,128)S(1)} %copy.41, pred[24,24]{1,0:T(8,128)(4,1)S(1)} %iota_compare_fusion.3, s32[8,8,24]{2,1,0:T(8,128)S(1)} %copy.39), kind=kLoop, calls=%fused_computation | loop fusion | flops 291840 | bytes 25152 | tf_op jit(solution)/shard_map/reduce_sum | solution.py:485
  27.8 0.6 reduce_max.18
  29.1 0.6 reduce_max.19
  30.5 0.2 select_reduce_fusion.3
  30.8 0.1 reshape.207
  30.9 0.3 select_reduce_fusion.1
  31.2 0.1 reshape.209
  31.3 0.1 reshape.208
  31.4 0.1 reshape.210
  31.6 0.4 select_reduce_fusion
  32.0 0.1 copy.44
  32.1 0.1 reshape.211
  32.3 164.9 %conditional.1 = ((bf16[4,128,128]{2,1,0:T(8,128)(2,1)S(1)}, bf16[32,128]{1,0:T(8,128)(2,1)S(1)}, bf16[24,128,128]{2,1,0:T(8,128)(2,1)S(1)}, bf16[24,32,128]{2,1,0:T(8,128)(2,1)S(1)})) conditional(s32[]{:T(128)} %clamp.9, (bf16[1,16,16,128,128]{4,3,2,1,0:T(8,128)(2,1)}, bf16[1,2048,128]{2,1,0:T(8,128)(2,1)}, ...), branch_computations={%region_9.10_spmd, %region_10.11_spmd, %region_11.12_spmd, %region... | conditional | bytes 8 | solution.py:539
  32.3 164.6 %branch_0_fun.1 = (bf16[4,128,128]{2,1,0:T(8,128)(2,1)S(1)}, bf16[32,128]{1,0:T(8,128)(2,1)S(1)}, bf16[24,128,128]{2,1,0:T(8,128)(2,1)S(1)}, bf16[24,32,128]{2,1,0:T(8,128)(2,1)S(1)}) custom-call(s32[568]{0:T(1024)S(1)} %get-tuple-element.83.table, bf16[24,128,128]{2,1,0:T(8,128)(2,1)} %get-tuple-element.169.panel, bf16[16,16,128,128]{3,2,1,0:T(8,128)(2,1)} %bitcast.38, ...), custom_call_target="tpu_custom_call" | custom-call | tf_op jit(solution)/shard_map/cond/branch_0_fun/pallas_call | solution.py:425
  197.2 0.7 copy.71
  197.8 0.6 copy.72
  198.4 0.9 copy.73
  199.3 0.7 copy.74
  (21 shorter events, 0.4 us)

commit v4 on v3

--- a/solution.py
+++ b/solution.py
@@ -18,17 +18,19 @@
 F32 = jnp.float32
 
 
-STEPS = (0, 4, 2, 6, 1, 7, 3, 5)
+STEPS = (0, 1, 7, 4, 3, 5, 2, 6)
 AT_ONCE = 3
 PICKS = NXC * CAP
 PAIR = CORES * CAP
 SIZES = ((6, 3), (7, 3), (8, 3), (PICKS, PAIR))
 Z_CHILD = 0
-X_PICK = Z_CHILD + NZ * PICKS
-Z_PICK = X_PICK + NZ * PICKS
-SPOTS = Z_PICK + NZ * PICKS
+X_PICK = Z_CHILD + NZ
+Z_PICK = X_PICK + NZ
+SPOTS = Z_PICK + NZ
+SLOT = SPOTS + NXC
+SIZE = SLOT + 8
 SPOT = 1 + NB
-SLOT = SPOTS + NXC * PAIR * SPOT
+LANES = 128
 
 
 def place():
@@ -42,8 +44,10 @@
     )
 
 
-def routes_kernel(meta, out, send_sem, near_sem, far_sem):
+def routes_kernel(route, pattern, table, meta, out, send_sem, near_sem, far_sem):
     z, xc, k = place()
+    cx, core = lax.div(xc, CORES), lax.rem(xc, CORES)
+    count = route.shape[0]
 
     def mate_z(d):
         return lax.rem(z + d, NZ) * NXC + xc
@@ -55,6 +59,24 @@
         signal(mate_z(d), k)
     for d in range(1, NXC):
         signal(mate_xc(d), k)
+
+    fields = jnp.concatenate(
+        [route[...], pattern[...], jnp.zeros((count, LANES - SPOT), jnp.int32)], axis=1
+    )
+    fields = jnp.concatenate([fields, jnp.zeros((LANES - count, LANES), jnp.int32)], axis=0)
+    fields = fields.T[:8]
+    lane = lax.broadcasted_iota(jnp.int32, (8, LANES), 1)
+    low = lax.broadcasted_iota(jnp.int32, (8, LANES), 0)
+    real = lane < count
+    own = jnp.broadcast_to(fields[:1], (8, LANES))
+    goal, chip = own // NXC, own // CORES
+    spot, rank = jnp.zeros_like(own), jnp.zeros_like(own)
+    for j in range(count):
+        later = lane > j
+        spot += (later & (goal == goal[:, j : j + 1])).astype(jnp.int32)
+        rank += (later & (chip == chip[:, j : j + 1])).astype(jnp.int32)
+    spot, rank = jnp.where(real, spot, 0), jnp.where(real, rank, 0)
+    meta[...] = jnp.where(low == SPOT, spot, jnp.where(low == SPOT + 1, rank, fields))
     pl.semaphore_wait(pltpu.get_barrier_semaphore(), NZ + NXC - 2)
 
     pltpu.make_async_copy(meta, out.at[xc, z], near_sem).start()
@@ -67,6 +89,13 @@
             device_id=(mate_z(d), k),
             device_id_type=MESH,
         ).start()
+
+    z_child = jnp.zeros((NZ, LANES), jnp.int32)
+    for j in range(count):
+        col = slice(j, j + 1)
+        z_child += jnp.where((goal[:, col] == low) & (spot[:, col] == lane), j, 0)
+    table[Z_CHILD : Z_CHILD + NZ] = z_child
+
     pltpu.make_async_copy(out.at[xc], out.at[xc], near_sem).wait()
     for d in range(1, NXC):
         pltpu.make_async_remote_copy(
@@ -83,21 +112,76 @@
     pltpu.make_async_copy(part, part, send_sem.at[0]).wait()
     pltpu.make_async_copy(some, some, send_sem.at[1]).wait()
 
-
-def all_routes(meta):
+    most = out[0, 0]
+    for q in range(1, NXC * NZ):
+        most = jnp.maximum(most, out[q // NZ, q % NZ])
+    fullest = jnp.max(most[SPOT : SPOT + 1], axis=1, keepdims=True) + 1
+    widest = jnp.max(most[SPOT + 1 : SPOT + 2], axis=1, keepdims=True) + 1
+    size = jnp.full((1, 1), len(SIZES) - 1, jnp.int32)
+    slots = jnp.full((1, 1), SIZES[-1][0], jnp.int32)
+    lanes = jnp.full((1, 1), SIZES[-1][1], jnp.int32)
+    for i in reversed(range(len(SIZES) - 1)):
+        fits = (fullest <= SIZES[i][0]) & (widest <= SIZES[i][1])
+        size = jnp.where(fits, i, size)
+        slots = jnp.where(fits, SIZES[i][0], slots)
+        lanes = jnp.where(fits, SIZES[i][1], lanes)
+
+    table[SLOT : SLOT + 8] = goal * slots + spot
+
+    def rows(field):
+        return jnp.concatenate([out[xc, q, field : field + 1] for q in range(NZ)], axis=0)
+
+    there, spot, rank = rows(0), rows(SPOT), rows(SPOT + 1)
+    goal, chip = there // NXC, there // CORES % NX
+    x_key = jnp.where(goal == z, chip * PAIR + rank, -1)
+    z_key = jnp.where(goal == z, spot, -1)
+    z_value = chip * lanes + rank
+    x_pick = jnp.zeros((NZ, LANES), jnp.int32)
+    z_pick = jnp.zeros((NZ, LANES), jnp.int32)
+    for j in range(count):
+        col = slice(j, j + 1)
+        x_pick += jnp.where(x_key[:, col] == lane, spot[:, col], 0)
+        z_pick += jnp.where(z_key[:, col] == lane, z_value[:, col], 0)
+    table[X_PICK : X_PICK + NZ] = x_pick
+    table[Z_PICK : Z_PICK + NZ] = z_pick
+
+    turn = core * NB + lax.rem(k - cx + NB, NB)
+    step = jnp.int32(0)
+    for i in range(NZ):
+        step = jnp.where(turn == i, STEPS[i], step)
+    source = lax.rem(z - step + NZ, NZ)
+    there = [
+        jnp.concatenate([out[q, source, f : f + 1] for q in range(NXC)], axis=0)
+        for f in (*range(SPOT), SPOT + 1)
+    ]
+    chip, rank = there[0] // CORES, there[SPOT]
+    key = jnp.where(chip == z * NX + cx, rank * SPOT, -SPOT)
+    values = [(there[0] % CORES != core).astype(jnp.int32)] + there[1:SPOT]
+    spots = jnp.zeros((NXC, LANES), jnp.int32)
+    for j in range(count):
+        col = slice(j, j + 1)
+        for f in range(SPOT):
+            spots += jnp.where(key[:, col] + f == lane, values[f][:, col], 0)
+    table[SPOTS : SPOTS + NXC] = spots
+    table[SIZE : SIZE + 8] = jnp.broadcast_to(size, (8, LANES))
+
+
+def tables(route, pattern):
     vmem = pl.BlockSpec(memory_space=pltpu.VMEM)
     return pl.pallas_call(
         routes_kernel,
-        out_shape=jax.ShapeDtypeStruct((NXC, NZ) + meta.shape, meta.dtype),
-        in_specs=[vmem],
+        out_shape=jax.ShapeDtypeStruct((SIZE + 8, LANES), jnp.int32),
+        in_specs=[vmem, vmem],
         out_specs=vmem,
         scratch_shapes=[
+            pltpu.VMEM((8, LANES), jnp.int32),
+            pltpu.VMEM((NXC, NZ, 8, LANES), jnp.int32),
             pltpu.SemaphoreType.DMA((2,)),
             pltpu.SemaphoreType.DMA,
             pltpu.SemaphoreType.DMA,
         ],
         compiler_params=pltpu.CompilerParams(collective_id=1, has_side_effects=True),
-    )(meta)
+    )(route, pattern)
 
 
 def greet():
@@ -189,7 +273,7 @@
 
     def launch(n):
         def fill(j, carry):
-            z_send[n, j] = panel[table[Z_CHILD + ahead(n) * PICKS + j]]
+            z_send[n, j] = panel[table[Z_CHILD + ahead(n), j]]
             return carry
 
         lax.fori_loop(0, slots, fill, 0)
@@ -199,7 +283,7 @@
         launch(n)
 
     def own(j, carry):
-        z_got[0][j] = panel[table[Z_CHILD + z * PICKS + j]]
+        z_got[0][j] = panel[table[Z_CHILD + z, j]]
         return carry
 
     lax.fori_loop(0, slots, own, 0)
@@ -212,7 +296,7 @@
             other = lax.rem(cx + o, NX)
             row = lax.rem(other + n, NB)
             for lane in range(lanes):
-                pick = table[X_PICK + behind(n) * PICKS + other * PAIR + lane]
+                pick = table[X_PICK + behind(n), other * PAIR + lane]
                 x_send[n * NX + other, lane] = z_got[n][pick]
             here = jnp.logical_and(o == 0, jnp.logical_and(core == n // NB, k == row))
 
@@ -275,9 +359,8 @@
             other = lax.rem(xc + o, NXC)
             pltpu.make_async_copy(x.at[other], x.at[other], xr_sem.at[other]).wait()
             for lane in range(lanes):
-                base = SPOTS + (other * PAIR + lane) * SPOT
-                which = table[base]
-                spot = [table[base + 1 + l] for l in range(NB)]
+                which = table[SPOTS + other, lane * SPOT]
+                spot = [table[SPOTS + other, lane * SPOT + 1 + l] for l in range(NB)]
                 right = jnp.concatenate([x[other, l, lane] for l in range(NB)], axis=0)
                 for i in range(NB):
                     left = jnp.concatenate(
@@ -324,13 +407,13 @@
 
     def backward(n):
         half, first = n // NB, n % NB * NX * lanes
-        if n % NB == 0:
+        if n in (3, 4):
             pltpu.make_async_copy(y_got[half], y_got[half], yr_sem.at[half]).wait()
         if n:
             z_copy(n).wait_send()
 
         def pack(j, carry):
-            block = y_got[half][first + table[Z_PICK + behind(n) * PICKS + j]]
+            block = y_got[half][first + table[Z_PICK + behind(n), j]]
             if n:
                 z_send[n, j] = block
             else:
@@ -359,7 +442,7 @@
     def _():
         children(1)
 
-    for n in range(NZ):
+    for n in (3, 2, 1, 0, 4, 5, 6, 7):
         backward(n)
     for n in range(1, NZ):
         home_copy(n, ahead(n)).wait_recv()
@@ -380,7 +463,7 @@
     for b in range(NB):
 
         def unpack(i, carry):
-            block = z_home[table[SLOT + i]]
+            block = z_home[table[SLOT, i]]
             column[i] = block
             term = lax.dot_general(
                 panel[i], block, (((0,), (0,)), ((), ())), preferred_element_type=F32
@@ -469,77 +552,17 @@
     )(table, panel_blocks, anc, parent_blocks, dinv, child_dinv)
 
 
-def tables(child_route, child_pattern):
-    z, xc, k = place()
-    cx, core = lax.div(xc, CORES), lax.rem(xc, CORES)
-    count = child_route.shape[0]
-    meta = jnp.concatenate([child_route.reshape(-1), child_pattern.T.reshape(-1)])
-    meta = jnp.pad(meta, (0, 8 * 128 - meta.shape[0])).reshape(8, 128)
-    meta = all_routes(meta).reshape(NXC, NZ, -1)[..., : (1 + NB) * count]
-    route = meta[..., :count]
-    pattern = meta[..., count:].reshape(NXC, NZ, NB, count)
-    goal = route // NXC
-    earlier = jnp.arange(count)[None, :] < jnp.arange(count)[:, None]
-    spot = jnp.sum(((goal[..., :, None] == goal[..., None, :]) & earlier).astype(jnp.int32), -1)
-    chip = route // CORES
-    rank = jnp.sum(((chip[..., :, None] == chip[..., None, :]) & earlier).astype(jnp.int32), -1)
-    fullest, widest = jnp.max(spot) + 1, jnp.max(rank) + 1
-
-    def of_xc(values):
-        return lax.dynamic_index_in_dim(values, xc, 0, keepdims=False)
-
-    places = jnp.arange(PICKS, dtype=jnp.int32)[:, None]
-    route_xc, spot_xc, rank_xc = of_xc(route), of_xc(spot), of_xc(rank)
-    goal_xc = route_xc // NXC
-    own_goal = lax.dynamic_index_in_dim(goal_xc, z, 0, keepdims=False)
-    own_spot = lax.dynamic_index_in_dim(spot_xc, z, 0, keepdims=False)
-    hit = (own_goal == jnp.arange(NZ)[:, None, None]) & (own_spot == places)
-    z_child = jnp.sum(jnp.where(hit, jnp.arange(count, dtype=jnp.int32), 0), -1)
-
-    mine = (goal_xc == z)[:, None]
-    lane_xc = rank_xc[:, None]
-    chip_xc = (route_xc // CORES % NX)[:, None]
-    via = spot_xc[:, None]
-    x_pick = jnp.sum(jnp.where(mine & (chip_xc * PAIR + lane_xc == places), via, 0), -1)
-
-    turn = core * NB + lax.rem(k - cx + NB, NB)
-    step = jnp.sum(jnp.where(jnp.arange(NZ) == turn, jnp.array(STEPS, jnp.int32), 0))
-    source = lax.rem(z - step + NZ, NZ)
-
-    def of_source(values):
-        return lax.dynamic_index_in_dim(values, source, 1, keepdims=False)
-
-    there, lane = of_source(route), of_source(rank)
-    hit = (there // CORES == z * NX + cx)[:, None] & (lane[:, None] == jnp.arange(PAIR)[:, None])
-    which = (there % CORES != core).astype(jnp.int32)
-    spots = jnp.concatenate([which[:, None], of_source(pattern)], axis=1)
-    spots = jnp.sum(jnp.where(hit[:, :, None], spots[:, None], 0), -1)
-
-    def with_slots(slots, lanes):
-        z_pick = jnp.sum(jnp.where(mine & (via == places), chip_xc * lanes + lane_xc, 0), -1)
-        parts = (z_child, x_pick, z_pick, spots, own_goal * slots + own_spot)
-        return jnp.concatenate([part.reshape(-1) for part in parts])
-
-    return fullest, widest, with_slots
-
-
 def on_device(
     anc_inverse, parent_panel, parent_dinv, child_route, child_pattern, child_panel, child_dinv
 ):
     width = parent_dinv.shape[-1]
     ancestors = anc_inverse.shape[1]
     count = child_route.shape[0]
-    fullest, widest, with_slots = tables(child_route, child_pattern)
-    fits = [(fullest <= slots) & (widest <= lanes) for slots, lanes in SIZES[:-1]]
-    size = jnp.int32(len(SIZES) - 1)
-    for i in reversed(range(len(fits))):
-        size = jnp.where(fits[i], i, size)
-    slots = sum(jnp.where(size == i, SIZES[i][0], 0) for i in range(len(SIZES)))
-    lanes = sum(jnp.where(size == i, SIZES[i][1], 0) for i in range(len(SIZES)))
+    table = tables(child_route, child_pattern)
     below, diag, column, child_diag = lax.switch(
-        size,
+        table[SIZE, 0],
         [functools.partial(whole, *SIZES[i], 2 + i) for i in range(len(SIZES))],
-        with_slots(slots, lanes),
+        table,
         child_panel.reshape(count, width, width),
         anc_inverse[0],
         parent_panel[0].reshape(ancestors, width, width),

time: 200 us -> 177 us (0.89); the launches traced: 200 us -> 174 us
  Pallas kernels: 184 us -> 166 us
  other arithmetic: 7.23 us -> 0 us
    pallas_call x1, Pallas kernels: 165 us -> 147 us  [whole(): pl.pallas_call(functools.partial(whole_kernel, slots, lanes), out_shape=(...]
    reduce_sum x5 -> x0, other arithmetic: 5.05 us -> none  [the longest x1 2.78 us: tables(): jnp.sum(((chip[..., :, None] == chip[..., None, :]) & earlier).astype(jnp...]
    reshape x8 -> x0, local copies, waits for them, and re-layouts: 2.84 us -> none  [the longest x1 1 us: tables(): meta = all_routes(meta).reshape(NXC, NZ, -1)[..., :(1 + NB) * count]]
    unnamed x4 -> x6, local copies, waits for them, and re-layouts: 2.81 us -> 5.5 us
where the time goes in v4:
time: 177 us; the launch traced here: 174 us
  Pallas kernels  166 us (94%)
  local copies, waits for them, and re-layouts  6.02 us (3%)
    pallas_call x1, Pallas kernels, whole(): pl.pallas_call(functools.partial(whole_kernel, slots, lanes), out_shape=(...  147 us
    pallas_call x1, Pallas kernels, tables(): pl.pallas_call(routes_kernel, out_shape=jax.ShapeDtypeStruct((SIZE + 8, L...  19 us
    unnamed x6, local copies, waits for them, and re-layouts  5.5 us

profile of v4, /device:TPU:1, one launch (start us, length us, event | category | flops | bytes accessed | tf_op | source)
XLA Modules:
  0.0 173.9 jit_solution(17079524224634194484)
XLA Ops:
  0.6 1.3 copy.11.route
  2.0 1.4 copy.12.pattern
  3.3 19.0 %shard_map.102 = s32[48,128]{1,0:T(8,128)S(1)} custom-call(s32[24,1]{1,0:T(8,128)} %copy.11.route, s32[24,4]{1,0:T(8,128)} %copy.12.pattern), custom_call_target="tpu_custom_call" | custom-call | tf_op jit(solution)/shard_map/pallas_call | solution.py:171
  22.3 0.5 slice.3
  23.5 147.6 %conditional.1 = ((bf16[4,128,128]{2,1,0:T(8,128)(2,1)S(1)}, bf16[32,128]{1,0:T(8,128)(2,1)S(1)}, bf16[24,128,128]{2,1,0:T(8,128)(2,1)S(1)}, bf16[24,32,128]{2,1,0:T(8,128)(2,1)S(1)})) conditional(s32[]{:T(128)} %bitcast, (s32[48,128]{1,0:T(8,128)S(1)}, bf16[24,128,128]{2,1,0:T(8,128)(2,1)}, ...), branch_computations={%region_0.0_spmd, %region_1.0_spmd, %region_2.0_spmd, %region_3.0_... | conditional | bytes 8 | solution.py:562
  23.7 147.2 %branch_1_fun.1 = (bf16[4,128,128]{2,1,0:T(8,128)(2,1)S(1)}, bf16[32,128]{1,0:T(8,128)(2,1)S(1)}, bf16[24,128,128]{2,1,0:T(8,128)(2,1)S(1)}, bf16[24,32,128]{2,1,0:T(8,128)(2,1)S(1)}) custom-call(s32[48,128]{1,0:T(8,128)S(1)} %get-tuple-element.77.table, bf16[24,128,128]{2,1,0:T(8,128)(2,1)} %get-tuple-element.78.panel, ...), custom_call_target="tpu_custom_call" | custom-call | tf_op jit(solution)/shard_map/cond/branch_1_fun/pallas_call | solution.py:508
  171.1 0.7 copy.33
  171.7 0.6 copy.34
  172.3 0.9 copy.35
  173.2 0.7 copy.36

commit v5 on v4

--- a/solution.py
+++ b/solution.py
@@ -18,7 +18,7 @@
 F32 = jnp.float32
 
 
-STEPS = (0, 1, 7, 4, 3, 5, 2, 6)
+STEPS = (0, 1, 7, 4, 2, 6, 3, 5)
 AT_ONCE = 3
 PICKS = NXC * CAP
 PAIR = CORES * CAP
@@ -407,7 +407,7 @@
 
     def backward(n):
         half, first = n // NB, n % NB * NX * lanes
-        if n in (3, 4):
+        if n in (3, 6):
             pltpu.make_async_copy(y_got[half], y_got[half], yr_sem.at[half]).wait()
         if n:
             z_copy(n).wait_send()
@@ -442,7 +442,7 @@
     def _():
         children(1)
 
-    for n in (3, 2, 1, 0, 4, 5, 6, 7):
+    for n in (3, 2, 1, 0, 6, 7, 4, 5):
         backward(n)
     for n in range(1, NZ):
         home_copy(n, ahead(n)).wait_recv()

time: 177 us -> 189 us (1.068)
  the two profiles are of different devices: /device:TPU:1 before, /device:TPU:96 now
where the time goes in v5:
time: 189 us
  Pallas kernels  181 us (96%)
  local copies, waits for them, and re-layouts  6.02 us (3%)
    pallas_call x1, Pallas kernels, whole(): pl.pallas_call(functools.partial(whole_kernel, slots, lanes), out_shape=(...  166 us
    pallas_call x1, Pallas kernels, tables(): pl.pallas_call(routes_kernel, out_shape=jax.ShapeDtypeStruct((SIZE + 8, L...  15 us
    unnamed x6, local copies, waits for them, and re-layouts  5.5 us

profile of v5, /device:TPU:96, one launch (start us, length us, event | category | flops | bytes accessed | tf_op | source)
XLA Modules:
  0.0 188.8 jit_solution(5374155810564363447)
XLA Ops:
  0.6 1.3 copy.11.route
  2.0 1.4 copy.12.pattern
  3.3 15.0 %shard_map.102 = s32[48,128]{1,0:T(8,128)S(1)} custom-call(s32[24,1]{1,0:T(8,128)} %copy.11.route, s32[24,4]{1,0:T(8,128)} %copy.12.pattern), custom_call_target="tpu_custom_call" | custom-call | tf_op jit(solution)/shard_map/pallas_call | solution.py:171
  18.4 0.5 slice.3
  19.5 166.5 %conditional.1 = ((bf16[4,128,128]{2,1,0:T(8,128)(2,1)S(1)}, bf16[32,128]{1,0:T(8,128)(2,1)S(1)}, bf16[24,128,128]{2,1,0:T(8,128)(2,1)S(1)}, bf16[24,32,128]{2,1,0:T(8,128)(2,1)S(1)})) conditional(s32[]{:T(128)} %bitcast, (s32[48,128]{1,0:T(8,128)S(1)}, bf16[24,128,128]{2,1,0:T(8,128)(2,1)}, ...), branch_computations={%region_0.0_spmd, %region_1.0_spmd, %region_2.0_spmd, %region_3.0_... | conditional | bytes 8 | solution.py:562
  19.6 166.2 %branch_0_fun.1 = (bf16[4,128,128]{2,1,0:T(8,128)(2,1)S(1)}, bf16[32,128]{1,0:T(8,128)(2,1)S(1)}, bf16[24,128,128]{2,1,0:T(8,128)(2,1)S(1)}, bf16[24,32,128]{2,1,0:T(8,128)(2,1)S(1)}) custom-call(s32[48,128]{1,0:T(8,128)S(1)} %get-tuple-element.71.table, bf16[24,128,128]{2,1,0:T(8,128)(2,1)} %get-tuple-element.72.panel, ...), custom_call_target="tpu_custom_call" | custom-call | tf_op jit(solution)/shard_map/cond/branch_0_fun/pallas_call | solution.py:508
  186.0 0.7 copy.33
  186.7 0.6 copy.34
  187.3 0.9 copy.35
  188.2 0.7 copy.36

commit v6 on v4

--- a/solution.py
+++ b/solution.py
@@ -47,7 +47,7 @@
 def routes_kernel(route, pattern, table, meta, out, send_sem, near_sem, far_sem):
     z, xc, k = place()
     cx, core = lax.div(xc, CORES), lax.rem(xc, CORES)
-    count = route.shape[0]
+    count = route.shape[1]
 
     def mate_z(d):
         return lax.rem(z + d, NZ) * NXC + xc
@@ -60,11 +60,10 @@
     for d in range(1, NXC):
         signal(mate_xc(d), k)
 
-    fields = jnp.concatenate(
-        [route[...], pattern[...], jnp.zeros((count, LANES - SPOT), jnp.int32)], axis=1
-    )
-    fields = jnp.concatenate([fields, jnp.zeros((LANES - count, LANES), jnp.int32)], axis=0)
-    fields = fields.T[:8]
+    meta[...] = jnp.zeros_like(meta)
+    meta[0:1, :count] = route[...]
+    meta[1:SPOT, :count] = pattern[...]
+    fields = meta[...]
     lane = lax.broadcasted_iota(jnp.int32, (8, LANES), 1)
     low = lax.broadcasted_iota(jnp.int32, (8, LANES), 0)
     real = lane < count
@@ -558,7 +557,7 @@
     width = parent_dinv.shape[-1]
     ancestors = anc_inverse.shape[1]
     count = child_route.shape[0]
-    table = tables(child_route, child_pattern)
+    table = tables(child_route.T, child_pattern.T)
     below, diag, column, child_diag = lax.switch(
         table[SIZE, 0],
         [functools.partial(whole, *SIZES[i], 2 + i) for i in range(len(SIZES))],

time: 177 us -> 189 us (1.068); the launches traced: 174 us -> 189 us
  Pallas kernels: 166 us -> 184 us
  local copies, waits for them, and re-layouts: 6.02 us -> 3.32 us
    pallas_call x1, Pallas kernels: 147 us -> 165 us  [whole(): pl.pallas_call(functools.partial(whole_kernel, slots, lanes), out_shape=(...]
    unnamed x6 -> x4, local copies, waits for them, and re-layouts: 5.5 us -> 2.81 us
where the time goes in v6:
time: 189 us
  Pallas kernels  184 us (97%)
  local copies, waits for them, and re-layouts  3.32 us (2%)
    pallas_call x1, Pallas kernels, whole(): pl.pallas_call(functools.partial(whole_kernel, slots, lanes), out_shape=(...  165 us
    pallas_call x1, Pallas kernels, tables(): pl.pallas_call(routes_kernel, out_shape=jax.ShapeDtypeStruct((SIZE + 8, L...  19.1 us

profile of v6, /device:TPU:1, one launch (start us, length us, event | category | flops | bytes accessed | tf_op | source)
XLA Modules:
  0.0 189.4 jit_solution(14704228376690770672)
XLA Ops:
  0.6 19.1 %shard_map.102 = s32[48,128]{1,0:T(8,128)S(1)} custom-call(s32[1,24]{1,0:T(1,128)} %bitcast.23, s32[4,24]{1,0:T(4,128)} %bitcast.22), custom_call_target="tpu_custom_call" | custom-call | tf_op jit(solution)/shard_map/pallas_call | solution.py:170
  19.7 0.5 slice.3
  20.9 165.6 %conditional.1 = ((bf16[4,128,128]{2,1,0:T(8,128)(2,1)S(1)}, bf16[32,128]{1,0:T(8,128)(2,1)S(1)}, bf16[24,128,128]{2,1,0:T(8,128)(2,1)S(1)}, bf16[24,32,128]{2,1,0:T(8,128)(2,1)S(1)})) conditional(s32[]{:T(128)} %bitcast.2, (s32[48,128]{1,0:T(8,128)S(1)}, bf16[24,128,128]{2,1,0:T(8,128)(2,1)}, ...), branch_computations={%region_0.0_spmd, %region_1.0_spmd, %region_2.0_spmd, %region_3.0_... | conditional | bytes 8 | solution.py:561
  20.9 165.4 %branch_0_fun.1 = (bf16[4,128,128]{2,1,0:T(8,128)(2,1)S(1)}, bf16[32,128]{1,0:T(8,128)(2,1)S(1)}, bf16[24,128,128]{2,1,0:T(8,128)(2,1)S(1)}, bf16[24,32,128]{2,1,0:T(8,128)(2,1)S(1)}) custom-call(s32[48,128]{1,0:T(8,128)S(1)} %get-tuple-element.71.table, bf16[24,128,128]{2,1,0:T(8,128)(2,1)} %get-tuple-element.72.panel, ...), custom_call_target="tpu_custom_call" | custom-call | tf_op jit(solution)/shard_map/cond/branch_0_fun/pallas_call | solution.py:507
  186.5 0.7 copy.31
  187.2 0.6 copy.32
  187.8 0.9 copy.33
  188.7 0.7 copy.34
